TPU v7x, 128 devices: a whole 4x4x4 slice. The times are simulated.
128 devices in a mesh: group: 8 (over x, z_hi), replica: 16 (over z_lo, y, core).
Axes of the slice: x: 4, y: 4, z: 4 (z_hi: 2, z_lo: 2; z = z_hi * 2 + z_lo), core: 2. Of those that a mesh axis runs over, the one named last changes fastest.
Arguments:
- tokens: bfloat16 [32768, 1024], P(('group', 'replica')), may hold values from -24 to 24
- norm_gain: bfloat16 [1024], P('group'), may hold values from 0.25 to 1.75
- in_weight: bfloat16 [1024, 3072], P('group'), may hold values from -0.1875 to 0.1875
- conv_weight: bfloat16 [3, 1024], P(None, 'group'), may hold values from -3.5 to 3.5
- out_weight: bfloat16 [1024, 1024], P('group'), may hold values from -0.1875 to 0.1875
- ffn_gain: bfloat16 [1024], P('group'), may hold values from 0.25 to 1.75
- gate_weight: bfloat16 [1024, 4608], P('group'), may hold values from -0.1875 to 0.1875
- up_weight: bfloat16 [1024, 4608], P('group'), may hold values from -0.1875 to 0.1875
- down_weight: bfloat16 [4608, 1024], P('group'), may hold values from -0.1875 to 0.1875
- cotangent: bfloat16 [32768, 1024], P(('group', 'replica')), may hold values from -24 to 24
Outputs:
- block_out: bfloat16 [32768, 1024], P(('group', 'replica'))
- token_input_gradient: float32 [32768, 1024], P(('group', 'replica'))
- norm_gain_grad: float32 [1024], P('group')
- in_weight_grad: float32 [1024, 3072], P('group')
- conv_weight_grad: float32 [3, 1024], P(None, 'group')
- out_weight_grad: float32 [1024, 1024], P('group')
- ffn_gain_grad: float32 [1024], P('group')
- gate_weight_grad: float32 [1024, 4608], P('group')
- up_weight_grad: float32 [1024, 4608], P('group')
- down_weight_grad: float32 [4608, 1024], P('group')
All inputs are finite; a program needn't handle non-finite values.
Results may differ from a plain program's by a relative error of at most 0.018.
Values may be sent and summed in bfloat16 or wider, within the bound.
A program may use at most 256 MiB of HBM per device.

v0:
```python
import jax
import jax.numpy as jnp
from jax import lax
from jax.sharding import PartitionSpec as P

LENGTH = 2048


EPSILON = 1e-06


def passed_along(block, axis, distance):
    devices = range(lax.axis_size(axis))
    route = [(i - distance, i) for i in devices if i - distance in devices]
    return lax.ppermute(block, axis, route)


def rms_scale(value_entries):
    return lax.rsqrt(jnp.mean(value_entries * value_entries, axis=-1, keepdims=True) + EPSILON)


def norm_reverse(value_entries, scale, gain, grad):
    weighted = grad * gain
    return scale * weighted - value_entries * scale * scale * scale * jnp.mean(
        weighted * value_entries, axis=-1, keepdims=True
    )


def contract_rows(left, right):
    return lax.dot_general(
        left, right, (((0,), (0,)), ((), ())), preferred_element_type=jnp.float32
    )


def back_project(grad, weight_matrix):
    return lax.dot_general(
        grad, weight_matrix, (((1,), (1,)), ((), ())), preferred_element_type=jnp.float32
    )


def on_device(
    tokens,
    norm_gain,
    in_weight,
    conv_weight,
    out_weight,
    ffn_gain,
    gate_weight,
    up_weight,
    down_weight,
    cotangent,
):
    gain_one, w_in, w_conv, w_out, gain_two, w_gate, w_up, w_down = (
        lax.all_gather(norm_gain, "group", axis=0, tiled=True),
        lax.all_gather(in_weight, "group", axis=0, tiled=True),
        lax.all_gather(conv_weight, "group", axis=1, tiled=True),
        lax.all_gather(out_weight, "group", axis=0, tiled=True),
        lax.all_gather(ffn_gain, "group", axis=0, tiled=True),
        lax.all_gather(gate_weight, "group", axis=0, tiled=True),
        lax.all_gather(up_weight, "group", axis=0, tiled=True),
        lax.all_gather(down_weight, "group", axis=0, tiled=True),
    )
    tok_rows = tokens.shape[0]
    model_width = w_out.shape[0]
    first_pos = lax.axis_index(("group", "replica")) * tok_rows
    at_start = first_pos % LENGTH == 0
    at_end = (first_pos + tok_rows) % LENGTH == 0
    gain_first = gain_one.astype(jnp.float32)
    gain_second = gain_two.astype(jnp.float32)
    tap_zero = w_conv[0].astype(jnp.float32)
    tap_one = w_conv[1].astype(jnp.float32)
    tap_two = w_conv[2].astype(jnp.float32)
    hidden_input = tokens.astype(jnp.float32)
    scale_one = rms_scale(hidden_input)
    normed_one = (hidden_input * scale_one * gain_first).astype(jnp.bfloat16)
    projected = jnp.dot(normed_one, w_in, preferred_element_type=jnp.float32)
    b_part = projected[:, :model_width]
    c_part = projected[:, model_width : 2 * model_width]
    x_part = projected[:, 2 * model_width :]
    mixed_in = b_part * x_part
    rim_rows = passed_along(mixed_in[tok_rows - 2 :], "replica", 1)
    rim_rows = jnp.where(at_start, jnp.zeros_like(rim_rows), rim_rows)
    extended = jnp.concatenate([rim_rows, mixed_in], axis=0)
    conv_out = (
        tap_zero * extended[:tok_rows]
        + tap_one * extended[1 : tok_rows + 1]
        + tap_two * extended[2:]
    )
    gated = (c_part * conv_out).astype(jnp.bfloat16)
    middle = hidden_input + jnp.dot(gated, w_out, preferred_element_type=jnp.float32)
    scale_two = rms_scale(middle)
    normed_two = (middle * scale_two * gain_second).astype(jnp.bfloat16)
    gate_pre = jnp.dot(normed_two, w_gate, preferred_element_type=jnp.float32)
    up_pre = jnp.dot(normed_two, w_up, preferred_element_type=jnp.float32)
    gate_sigmoid = jax.nn.sigmoid(gate_pre)
    gate_act = gate_pre * gate_sigmoid
    hidden_act = (gate_act * up_pre).astype(jnp.bfloat16)
    block_out = (middle + jnp.dot(hidden_act, w_down, preferred_element_type=jnp.float32)).astype(
        jnp.bfloat16
    )
    cot_value = cotangent.astype(jnp.float32)
    d_wdown = contract_rows(hidden_act, cotangent)
    d_hidden = back_project(cotangent, w_down)
    d_gate = (d_hidden * up_pre * gate_sigmoid * (1.0 + gate_pre * (1.0 - gate_sigmoid))).astype(
        jnp.bfloat16
    )
    d_upper = (d_hidden * gate_act).astype(jnp.bfloat16)
    d_wgate = contract_rows(normed_two, d_gate)
    d_wup = contract_rows(normed_two, d_upper)
    d_normed_two = back_project(d_gate, w_gate) + back_project(d_upper, w_up)
    d_gain_two = jnp.sum(d_normed_two * middle * scale_two, axis=0)
    d_middle = cot_value + norm_reverse(middle, scale_two, gain_second, d_normed_two)
    d_branch = d_middle.astype(jnp.bfloat16)
    d_wout = contract_rows(gated, d_branch)
    d_gated = back_project(d_branch, w_out)
    d_cpart = d_gated * conv_out
    d_conv = d_gated * c_part
    next_rows = passed_along(d_conv[:2], "replica", -1)
    next_rows = jnp.where(at_end, jnp.zeros_like(next_rows), next_rows)
    after = jnp.concatenate([d_conv, next_rows], axis=0)
    d_mixed = tap_zero * after[2:] + tap_one * after[1 : tok_rows + 1] + tap_two * after[:tok_rows]
    d_wconv = jnp.stack(
        [
            jnp.sum(d_conv * extended[:tok_rows], axis=0),
            jnp.sum(d_conv * extended[1 : tok_rows + 1], axis=0),
            jnp.sum(d_conv * extended[2:], axis=0),
        ],
        axis=0,
    )
    d_projected = jnp.concatenate([d_mixed * x_part, d_cpart, d_mixed * b_part], axis=1).astype(
        jnp.bfloat16
    )
    d_win = contract_rows(normed_one, d_projected)
    d_normed_one = back_project(d_projected, w_in)
    d_gain_one = jnp.sum(d_normed_one * hidden_input * scale_one, axis=0)
    token_input_gradient = d_middle + norm_reverse(
        hidden_input, scale_one, gain_first, d_normed_one
    )
    grad_terms = (d_gain_one, d_win, d_wconv, d_wout, d_gain_two, d_wgate, d_wup, d_wdown)
    shares = (
        lax.psum_scatter(grad_terms[0], ("group", "replica"), scatter_dimension=0, tiled=True),
        lax.psum_scatter(grad_terms[1], ("group", "replica"), scatter_dimension=0, tiled=True),
        lax.psum_scatter(grad_terms[2], ("group", "replica"), scatter_dimension=1, tiled=True),
        lax.psum_scatter(grad_terms[3], ("group", "replica"), scatter_dimension=0, tiled=True),
        lax.psum_scatter(grad_terms[4], ("group", "replica"), scatter_dimension=0, tiled=True),
        lax.psum_scatter(grad_terms[5], ("group", "replica"), scatter_dimension=0, tiled=True),
        lax.psum_scatter(grad_terms[6], ("group", "replica"), scatter_dimension=0, tiled=True),
        lax.psum_scatter(grad_terms[7], ("group", "replica"), scatter_dimension=0, tiled=True),
    )
    owned = (
        lax.all_gather(shares[0].astype(jnp.bfloat16), "replica", axis=0, tiled=True).astype(
            jnp.float32
        ),
        lax.all_gather(shares[1].astype(jnp.bfloat16), "replica", axis=0, tiled=True).astype(
            jnp.float32
        ),
        lax.all_gather(shares[2].astype(jnp.bfloat16), "replica", axis=1, tiled=True).astype(
            jnp.float32
        ),
        lax.all_gather(shares[3].astype(jnp.bfloat16), "replica", axis=0, tiled=True).astype(
            jnp.float32
        ),
        lax.all_gather(shares[4].astype(jnp.bfloat16), "replica", axis=0, tiled=True).astype(
            jnp.float32
        ),
        lax.all_gather(shares[5].astype(jnp.bfloat16), "replica", axis=0, tiled=True).astype(
            jnp.float32
        ),
        lax.all_gather(shares[6].astype(jnp.bfloat16), "replica", axis=0, tiled=True).astype(
            jnp.float32
        ),
        lax.all_gather(shares[7].astype(jnp.bfloat16), "replica", axis=0, tiled=True).astype(
            jnp.float32
        ),
    )
    return (
        block_out,
        token_input_gradient,
        owned[0],
        owned[1],
        owned[2],
        owned[3],
        owned[4],
        owned[5],
        owned[6],
        owned[7],
    )


def solution(mesh):
    in_specs = (
        P(("group", "replica"), None),
        P("group"),
        P("group", None),
        P(None, "group"),
        P("group", None),
        P("group"),
        P("group", None),
        P("group", None),
        P("group", None),
        P(("group", "replica"), None),
    )
    out_specs = (
        P(("group", "replica"), None),
        P(("group", "replica"), None),
        P("group"),
        P("group", None),
        P(None, "group"),
        P("group", None),
        P("group"),
        P("group", None),
        P("group", None),
        P("group", None),
    )
    return jax.shard_map(
        on_device, mesh=mesh, in_specs=in_specs, out_specs=out_specs, check_vma=False
    )
```

profile of v0, /device:TPU:1, one launch (start us, length us, event | category | flops | bytes accessed | tf_op | source)
XLA Modules:
  0.0 2010.6 jit_solution(17919451139287745837)
XLA Ops:
  10.6 21.1 %all-gather = bf16[8,1,128]{2,1,0:T(2,128)(2,1)S(1)} all-gather(bf16[1,1,128]{2,1,0:T(2,128)(2,1)S(1)} %bitcast.63), channel_id=1, replica_groups=mesh['group'=8,'replica'=16] {'group'}, dimensions={0}, use_global_device_ids=true | all-gather | bytes 2304 | tf_op jit(solution)/shard_map/all_gather | solution.py:54
  31.8 14.6 all_gather.50
  46.6 56.3 %all-gather.13.cloned.1.call-done = bf16[1024,3072]{1,0:T(8,128)(2,1)} async-done(((bf16[128,3072]{1,0:T(8,128)(2,1)}), bf16[1024,3072]{1,0:T(8,128)(2,1)}) %all-gather.13.cloned.1.call-update) | async-done | bytes 6291472 | tf_op jit(solution)/shard_map/all_gather | solution.py:55
  113.3 14.9 all-gather.1
  132.0 25.0 %all-gather.15.cloned.1.call-done = bf16[1024,1024]{1,0:T(8,128)(2,1)} async-done(((bf16[128,1024]{1,0:T(8,128)(2,1)}), bf16[1024,1024]{1,0:T(8,128)(2,1)}) %all-gather.15.cloned.1.call-update) | async-done | bytes 2097168 | tf_op jit(solution)/shard_map/all_gather | solution.py:57
  159.9 117.6 %all-gather.17.cloned.1.call-done = bf16[1024,4608]{1,0:T(8,128)(2,1)} async-done(((bf16[128,4608]{1,0:T(8,128)(2,1)}), bf16[1024,4608]{1,0:T(8,128)(2,1)}) %all-gather.17.cloned.1.call-update) | async-done | bytes 9437200 | tf_op jit(solution)/shard_map/all_gather | solution.py:59
  277.5 8.0 fusion.35
  285.5 110.5 %all-gather.19.cloned.1.call-done = bf16[1024,4608]{1,0:T(8,128)(2,1)} async-done(((bf16[128,4608]{1,0:T(8,128)(2,1)}), bf16[1024,4608]{1,0:T(8,128)(2,1)}) %all-gather.19.cloned.1.call-update) | async-done | bytes 9437200 | tf_op jit(solution)/shard_map/all_gather | solution.py:60
  396.0 8.0 fusion.36
  404.0 110.5 %all-gather.21.cloned.1.call-done = bf16[4608,1024]{1,0:T(8,128)(2,1)} async-done(((bf16[576,1024]{1,0:T(8,128)(2,1)}), bf16[4608,1024]{1,0:T(8,128)(2,1)}) %all-gather.21.cloned.1.call-update) | async-done | bytes 9437200 | tf_op jit(solution)/shard_map/all_gather | solution.py:61
  514.5 13.8 multiply_convert_fusion
  537.9 9.9 fusion.39
  547.8 9.8 fusion.40
  557.6 369.5 %fusion = f32[40,1024]{1,0:T(8,128)S(1)} fusion(f32[4608,1024]{1,0:T(8,128)} %fusion.40), kind=kCustom, calls=%all-reduce-scatter | all-reduce-scatter fusion | flops 5242881 | bytes 19038208
  1016.3 15.1 reduce-scatter.14.cloned.1.call-done
  1045.8 64.5 %all-reduce.7 = (bf16[1024]{0:T(1024)(128)(2,1)S(1)}, bf16[3,1024]{1,0:T(4,128)(2,1)S(1)}, bf16[1024]{0:T(1024)(128)(2,1)S(1)}) all-reduce(f32[1024]{0:T(1024)S(1)} %get-tuple-element.15, f32[3,1024]{1,0:T(4,128)S(1)} %pad_maximum_fusion.5, ...), channel_id=2, replica_groups=mesh['group'=8,'replica'=16] {'group','replica'}, use_global_device_ids=true, to_apply=%region_5.6.clone | all-reduce | flops 5120 | bytes 30720
  1110.9 27.8 %all-reduce.8 = (bf16[128]{0:T(256)(128)(2,1)S(1)}, bf16[128]{0:T(256)(128)(2,1)S(1)}) all-reduce(bf16[128]{0:T(256)(128)(2,1)S(1)} %dynamic-update-slice, bf16[128]{0:T(256)(128)(2,1)S(1)} %dynamic-update-slice.1), channel_id=1, replica_groups=mesh['group'=8,'replica'=16] {'replica'}, use_global_device_ids=true, to_apply=%add | all-reduce | flops 256 | bytes 1024
  1139.3 16.6 all-gather.2
  1161.2 544.2 %reduce-scatter.10.cloned.1.call-done = f32[8,1024]{1,0:T(8,128)} async-done(((f32[1024,1024]{1,0:T(8,128)}), f32[8,1024]{1,0:T(8,128)}) %reduce-scatter.10.cloned.1.call-update) | async-done | bytes 32784 | tf_op jit(solution)/shard_map/reduce_scatter | solution.py:144
  1706.2 24.2 %all_gather.59 = bf16[128,1024]{1,0:T(8,128)(2,1)S(1)} all-gather(bf16[8,1024]{1,0:T(8,128)(2,1)S(1)} %convert_element_type.109), channel_id=1, replica_groups=mesh['group'=8,'replica'=16] {'replica'}, dimensions={0}, use_global_device_ids=true | all-gather | bytes 278528 | tf_op jit(solution)/shard_map/all_gather | solution.py:160
  1731.3 200.2 %reduce-scatter.8.cloned.1.call-done = f32[8,3072]{1,0:T(8,128)} async-done(((f32[1024,3072]{1,0:T(8,128)}), f32[8,3072]{1,0:T(8,128)}) %reduce-scatter.8.cloned.1.call-update) | async-done | bytes 98320 | tf_op jit(solution)/shard_map/reduce_scatter | solution.py:142
  1932.4 22.1 %all_gather.57 = bf16[128,3072]{1,0:T(8,128)(2,1)S(1)} all-gather(bf16[8,3072]{1,0:T(8,128)(2,1)S(1)} %convert_element_type.105), channel_id=1, replica_groups=mesh['group'=8,'replica'=16] {'replica'}, dimensions={0}, use_global_device_ids=true | all-gather | bytes 835584 | tf_op jit(solution)/shard_map/all_gather | solution.py:154
  1955.8 11.5 all-gather.23.cloned.1.call-done
  1970.2 30.7 %all-gather.25.cloned.1.call-done = bf16[128,4608]{1,0:T(8,128)(2,1)} async-done(((bf16[8,4608]{1,0:T(8,128)(2,1)}), bf16[128,4608]{1,0:T(8,128)(2,1)}) %all-gather.25.cloned.1.call-update) | async-done | bytes 1179664 | tf_op jit(solution)/shard_map/all_gather | solution.py:169
  (179 shorter events, 148.5 us)
Async XLA Ops:
  7.2 95.7 %all-gather.13.cloned.1.call-start = ((), (), s32[]{:S(2)}) async-start(), calls=%async_computation.4 | async-start | bytes 7077888 | tf_op jit(solution)/shard_map/all_gather | solution.py:55
  7.9 149.1 %all-gather.15.cloned.1.call-start = ((), (), s32[]{:S(2)}) async-start(), calls=%async_computation.5 | async-start | bytes 2359296 | tf_op jit(solution)/shard_map/all_gather | solution.py:57
  8.7 268.8 %all-gather.17.cloned.1.call-start = ((), (), s32[]{:S(2)}) async-start(), calls=%async_computation.6 | async-start | bytes 10616832 | tf_op jit(solution)/shard_map/all_gather | solution.py:59
  9.4 386.6 %all-gather.19.cloned.1.call-start = ((), (), s32[]{:S(2)}) async-start(), calls=%async_computation.7 | async-start | bytes 10616832 | tf_op jit(solution)/shard_map/all_gather | solution.py:60
  10.0 504.5 %all-gather.21.cloned.1.call-start = ((), (), s32[]{:S(2)}) async-start(), calls=%async_computation.8 | async-start | bytes 10616832 | tf_op jit(solution)/shard_map/all_gather | solution.py:61
  10.6 1002.6 %reduce-scatter.12.cloned.1.call-start = ((), (), s32[]{:S(2)}) async-start(), calls=%async_computation.11 | async-start | bytes 19021824 | tf_op jit(solution)/shard_map/reduce_scatter | solution.py:146
  109.1 19.1 collective-permute-start
  537.6 493.8 %reduce-scatter.14.cloned.1.call-start = ((), (), s32[]{:S(2)}) async-start(), calls=%async_computation.13 | async-start | bytes 19021824 | tf_op jit(solution)/shard_map/reduce_scatter | solution.py:147
  547.7 610.9 %all-gather.27.cloned.1.call-start = ((), (), s32[]{:S(2)}) async-start(), calls=%async_computation.15 | async-start | bytes 1392640 | tf_op jit(solution)/shard_map/all_gather | solution.py:172
  927.2 7.8 collective-permute-start.13
  928.5 7.9 collective-permute-start.12
  931.1 11.8 collective-permute-start.11
  932.4 17.4 collective-permute-start.10
  933.7 17.4 collective-permute-start.9
  935.0 21.6 %collective-permute-start.8 = (bf16[40,1024]{1,0:T(8,128)(2,1)S(1)}, bf16[40,1024]{1,0:T(8,128)(2,1)S(1)}, u32[]{:S(2)}, u32[]{:S(2)}) collective-permute-start(bf16[40,1024]{1,0:T(8,128)(2,1)S(1)} %convert.42), channel_id=1, source_target_pairs={{0,7},{1,8},{2,9},{3,10},{4,11},{5,12},{6,13},{7,14},{8,15},{9,16}... | collective-permute-start | bytes 245768
  936.3 21.6 %collective-permute-start.7 = (bf16[40,1024]{1,0:T(8,128)(2,1)S(1)}, bf16[40,1024]{1,0:T(8,128)(2,1)S(1)}, u32[]{:S(2)}, u32[]{:S(2)}) collective-permute-start(bf16[40,1024]{1,0:T(8,128)(2,1)S(1)} %convert.42), channel_id=1, source_target_pairs={{0,6},{1,7},{2,8},{3,9},{4,10},{5,11},{6,12},{7,13},{8,14},{9,15},... | collective-permute-start | bytes 245768
  943.0 17.6 collective-permute-start.6
  949.9 10.7 collective-permute-start.5
  951.2 9.7 collective-permute-start.4
  958.0 8.5 collective-permute-start.2
  973.2 732.3 %reduce-scatter.10.cloned.1.call-start = ((), (), s32[]{:S(2)}) async-start(), calls=%async_computation.10 | async-start | bytes 4227072 | tf_op jit(solution)/shard_map/reduce_scatter | solution.py:144
  989.1 942.4 %reduce-scatter.8.cloned.1.call-start = ((), (), s32[]{:S(2)}) async-start(), calls=%async_computation.9 | async-start | bytes 12681216 | tf_op jit(solution)/shard_map/reduce_scatter | solution.py:142
  1013.2 954.1 %all-gather.23.cloned.1.call-start = ((), (), s32[]{:S(2)}) async-start(), calls=%async_computation.12 | async-start | bytes 1253376 | tf_op jit(solution)/shard_map/all_gather | solution.py:166
  1014.8 986.1 %all-gather.25.cloned.1.call-start = ((), (), s32[]{:S(2)}) async-start(), calls=%async_computation.14 | async-start | bytes 1253376 | tf_op jit(solution)/shard_map/all_gather | solution.py:169
  (36 other events, 1455.3 us)
Sparse Core Ops, SparseCore 0:
  10.4 92.4 all-gather.12
  105.2 51.7 all-gather.14
  159.4 118.0 all-gather.16
  279.7 116.2 all-gather.18
  398.2 116.2 all-gather.20
  537.7 243.3 reduce-scatter.11
  787.3 244.0 reduce-scatter.13
  1033.1 32.7 all-gather.26
  1068.2 637.1 reduce-scatter.9
  1711.0 220.3 reduce-scatter.7
  1933.9 33.3 all-gather.22
  1968.9 31.8 all-gather.24
where the time goes:
time: 2010 us
  waiting for transfers between devices  1230 us (61%)
  blocking collectives  575 us (29%)
  matrix products  101 us (5%)
  starting transfers between devices  40 us (2%)
  other arithmetic  27.6 us (1%)
    reduce_scatter x1, waiting for transfers between devices, on_device(): lax.psum_scatter(grad_terms[3], ('group', 'replica'), scatter_dimension=0...  544 us
    unnamed x3, blocking collectives  462 us
    reduce_scatter x1, waiting for transfers between devices, on_device(): lax.psum_scatter(grad_terms[1], ('group', 'replica'), scatter_dimension=0...  200 us
    all_gather x1, waiting for transfers between devices, on_device(): lax.all_gather(gate_weight, 'group', axis=0, tiled=True)  118 us
    all_gather x1, waiting for transfers between devices, on_device(): lax.all_gather(up_weight, 'group', axis=0, tiled=True)  111 us
    all_gather x1, waiting for transfers between devices, on_device(): lax.all_gather(down_weight, 'group', axis=0, tiled=True)  111 us
    all_gather x1, waiting for transfers between devices, on_device(): lax.all_gather(in_weight, 'group', axis=0, tiled=True)  56.3 us
  transfers between devices with their start and end apart: 27, of which 14 were waited for; matrix products, arithmetic and copies ran while one was open for 24% of the time, Pallas kernels for 0%

commit v1 on v0

v1 whole, which is shorter than its diff:
```python
import functools

import jax
import jax.numpy as jnp
from jax import lax
from jax.experimental import pallas as pl
from jax.experimental.pallas import tpu as pltpu
from jax.sharding import PartitionSpec as P

MESH = pl.DeviceIdType.MESH
EPSILON = 1e-06
BF = jnp.bfloat16
F32 = jnp.float32
D = 1024
SEG = 72
PAD = 80
FS = 8 * PAD
TEAM = 8
ROWS = 256
T = TEAM * ROWS
VLIM = 60 * 2**20


def coords():
    group, replica = lax.axis_index("group"), lax.axis_index("replica")
    return group // 2, group % 2, replica // 8, (replica // 2) % 4, replica % 2


def device(x, zh, zl, y, c):
    return (x * 2 + zh, zl * 8 + y * 2 + c)


def remote(src, dst, send, recv, target):
    return pltpu.make_async_remote_copy(
        src_ref=src, dst_ref=dst, send_sem=send, recv_sem=recv, device_id=target, device_id_type=MESH
    )


def team_peers():
    x, zh, zl, y, c = coords()
    return [device(x, zh, zl, y, 1 - c)] + [device(x, zh, zl, (y + d) % 4, c) for d in (1, 2, 3)]


def group_peers():
    x, zh, zl, y, c = coords()
    return [
        device((x + dx) % 4, (zh + dz) % 2, zl, y, c)
        for dx in range(4)
        for dz in range(2)
        if (dx, dz) != (0, 0)
    ]


def z_peer():
    x, zh, zl, y, c = coords()
    return device(x, zh, 1 - zl, y, c)


def meet(peers):
    barrier = pltpu.get_barrier_semaphore()
    for peer in peers:
        pl.semaphore_signal(barrier, inc=1, device_id=peer, device_id_type=MESH)
    pl.semaphore_wait(barrier, len(peers))


class TeamGather:
    def __init__(self, src, slot, send, recv, local):
        x, zh, zl, y, c = coords()
        self.c, self.y = c, y
        sibling = device(x, zh, zl, y, 1 - c)
        me = 2 * y + c
        self.own = pltpu.make_async_copy(src, slot(me), local)
        self.pair = remote(src, slot(me), send.at[0], recv.at[0], sibling)
        self.out = [
            remote(src, slot(me), send.at[d], recv.at[d], device(x, zh, zl, (y + d) % 4, c))
            for d in (2, 1, 3)
        ]
        self.relay = []
        for d in (1, 3, 2):
            block = slot(2 * ((y + 4 - d) % 4) + c)
            self.relay.append(
                (
                    remote(src, block, send.at[d], recv.at[d], sibling),
                    remote(block, block, send.at[3 + d], recv.at[3 + d], sibling),
                )
            )

    def start(self):
        for copy in self.out:
            copy.start()
        self.pair.start()
        self.own.start()

    def finish(self):
        for arrived, onward in self.relay:
            arrived.wait_recv()
            onward.start()
        self.own.wait()
        self.pair.wait()
        for copy in self.out:
            copy.wait_send()
        for _, onward in self.relay:
            onward.wait()


class GroupGather:
    def __init__(self, src, slot, send, recv, local):
        x, zh, zl, y, c = coords()
        me = x * 2 + zh
        self.own = pltpu.make_async_copy(src, slot(me), local)
        self.out = [
            remote(src, slot(me), send.at[i], recv.at[i], peer) for i, peer in enumerate(group_peers())
        ]

    def start(self):
        for copy in self.out:
            copy.start()
        self.own.start()

    def finish(self):
        self.own.wait()
        for copy in self.out:
            copy.wait()


class GroupScatter:
    def __init__(self, block, land, send, recv):
        x, zh, zl, y, c = coords()
        self.out = []
        i = 0
        for dx in range(4):
            for dz in range(2):
                if (dx, dz) == (0, 0):
                    continue
                to = ((x + dx) % 4) * 2 + (zh + dz) % 2
                peer = device((x + dx) % 4, (zh + dz) % 2, zl, y, c)
                self.out.append(remote(block(to), land.at[i], send.at[i], recv.at[i], peer))
                i += 1

    def start(self):
        for copy in self.out:
            copy.start()

    def finish(self):
        for copy in self.out:
            copy.wait()


def gather_kernel(n_team, n_group, *refs):
    n = n_team + n_group
    srcs, dsts = refs[:n], refs[n : 2 * n]
    tsend, trecv, gsend, grecv, local = refs[2 * n :]
    peers = (team_peers() if n_team else []) + (group_peers() if n_group else [])
    meet(peers)
    jobs = []
    for i in range(n):
        src, dst = srcs[i], dsts[i]
        if i < n_team:
            if dst.shape[0] == TEAM:
                slot = lambda k, dst=dst: dst.at[k]
            else:
                slot = lambda k, dst=dst: dst.at[:, pl.ds(pl.multiple_of(k * 128, 128), 128)]
            jobs.append(TeamGather(src, slot, tsend.at[i], trecv.at[i], local.at[i]))
        else:
            j = i - n_team
            jobs.append(
                GroupGather(src, lambda k, dst=dst: dst.at[k], gsend.at[j], grecv.at[j], local.at[i])
            )
    for job in jobs:
        job.start()
    for job in jobs:
        job.finish()


def gather(team, group, collective_id, name):
    shapes = [
        jax.ShapeDtypeStruct((T, D) if a.shape == (T, 128) else (TEAM,) + a.shape, a.dtype) for a in team
    ]
    shapes += [jax.ShapeDtypeStruct((8,) + a.shape, a.dtype) for a in group]
    n = len(shapes)
    return pl.pallas_call(
        functools.partial(gather_kernel, len(team), len(group)),
        out_shape=shapes,
        in_specs=[pl.BlockSpec(memory_space=pl.ANY)] * n,
        out_specs=[pl.BlockSpec(memory_space=pl.ANY)] * n,
        scratch_shapes=[
            pltpu.SemaphoreType.DMA((max(len(team), 1), 7)),
            pltpu.SemaphoreType.DMA((max(len(team), 1), 7)),
            pltpu.SemaphoreType.DMA((max(len(group), 1), 7)),
            pltpu.SemaphoreType.DMA((max(len(group), 1), 7)),
            pltpu.SemaphoreType.DMA((n,)),
        ],
        compiler_params=pltpu.CompilerParams(
            collective_id=collective_id, has_side_effects=True, vmem_limit_bytes=VLIM
        ),
        name=name,
    )(*team, *group)


def team_sum_kernel(n, *refs):
    srcs, outs = refs[:n], refs[n : 2 * n]
    pair_land, mine, land, send, recv = refs[2 * n :]
    x, zh, zl, y, c = coords()
    sibling = device(x, zh, zl, y, 1 - c)
    meet(team_peers())
    pairs = [[None] * 4 for _ in range(n)]
    for i in range(n):
        for d in (2, 1, 3, 0):
            k = (y + d) % 4
            pairs[i][d] = remote(
                srcs[i].at[2 * k + 1 - c], pair_land.at[i, d], send.at[i, d], recv.at[i, d], sibling
            )
            pairs[i][d].start()
    outgoing = []
    for i in range(n):
        for d in (2, 1, 3, 0):
            k = (y + d) % 4
            pairs[i][d].wait()
            mine[i, d] = (srcs[i][2 * k + c].astype(F32) + pair_land[i, d].astype(F32)).astype(BF)
            if d:
                copy = remote(
                    mine.at[i, d],
                    land.at[i, d - 1],
                    send.at[i, 3 + d],
                    recv.at[i, 3 + d],
                    device(x, zh, zl, k, c),
                )
                copy.start()
                outgoing.append(copy)
    for i in range(n):
        for copy in outgoing[3 * i : 3 * i + 3]:
            copy.wait()
        outs[i][...] = (
            mine[i, 0].astype(F32) + land[i, 0].astype(F32) + land[i, 1].astype(F32) + land[i, 2].astype(F32)
        )


def team_sum(arrays, collective_id, name):
    n = len(arrays)
    return pl.pallas_call(
        functools.partial(team_sum_kernel, n),
        out_shape=[jax.ShapeDtypeStruct((ROWS, D), F32)] * n,
        in_specs=[pl.BlockSpec(memory_space=pltpu.VMEM)] * n,
        out_specs=[pl.BlockSpec(memory_space=pltpu.VMEM)] * n,
        scratch_shapes=[
            pltpu.VMEM((n, 4, ROWS, D), BF),
            pltpu.VMEM((n, 4, ROWS, D), BF),
            pltpu.VMEM((n, 3, ROWS, D), BF),
            pltpu.SemaphoreType.DMA((n, 7)),
            pltpu.SemaphoreType.DMA((n, 7)),
        ],
        compiler_params=pltpu.CompilerParams(
            collective_id=collective_id, has_side_effects=True, vmem_limit_bytes=VLIM
        ),
        name=name,
    )(*arrays)


def grad_sum_kernel(n, *refs):
    srcs, outs = refs[:n], refs[n : 2 * n]
    rest = refs[2 * n :]
    lands, sums, others = rest[:n], rest[n : 2 * n], rest[2 * n : 3 * n]
    gsend, grecv, zsend, zrecv, tsend, trecv, local = rest[3 * n :]
    x, zh, zl, y, c = coords()
    me = x * 2 + zh
    meet(group_peers() + [z_peer()] + team_peers())
    jobs = [
        GroupScatter(lambda k, s=srcs[i]: s.at[k], lands[i], gsend.at[i], grecv.at[i]) for i in range(n)
    ]
    for job in jobs:
        job.start()
    across = []
    for i in range(n):
        jobs[i].finish()
        total = srcs[i][me].astype(F32)
        for k in range(7):
            total += lands[i][k].astype(F32)
        sums[i][0] = total.astype(sums[i].dtype)
        copy = remote(sums[i].at[0], others[i], zsend.at[i], zrecv.at[i], z_peer())
        copy.start()
        across.append(copy)
    gathers = []
    for i in range(n):
        across[i].wait()
        sums[i][1] = (sums[i][0].astype(F32) + others[i][...].astype(F32)).astype(sums[i].dtype)
        job = TeamGather(
            sums[i].at[1], lambda k, o=outs[i]: o.at[k], tsend.at[i], trecv.at[i], local.at[i]
        )
        job.start()
        gathers.append(job)
    for job in gathers:
        job.finish()


def grad_sum(arrays, collective_id, name):
    n = len(arrays)
    return pl.pallas_call(
        functools.partial(grad_sum_kernel, n),
        out_shape=[jax.ShapeDtypeStruct(a.shape, a.dtype) for a in arrays],
        in_specs=[pl.BlockSpec(memory_space=pltpu.VMEM)] * n,
        out_specs=[pl.BlockSpec(memory_space=pltpu.VMEM)] * n,
        scratch_shapes=[pltpu.VMEM((7,) + a.shape[1:], a.dtype) for a in arrays]
        + [pltpu.VMEM((2,) + a.shape[1:], a.dtype) for a in arrays]
        + [pltpu.VMEM(a.shape[1:], a.dtype) for a in arrays]
        + [
            pltpu.SemaphoreType.DMA((n, 7)),
            pltpu.SemaphoreType.DMA((n, 7)),
            pltpu.SemaphoreType.DMA((n,)),
            pltpu.SemaphoreType.DMA((n,)),
            pltpu.SemaphoreType.DMA((n, 7)),
            pltpu.SemaphoreType.DMA((n, 7)),
            pltpu.SemaphoreType.DMA((n,)),
        ],
        compiler_params=pltpu.CompilerParams(
            collective_id=collective_id, has_side_effects=True, vmem_limit_bytes=VLIM
        ),
        name=name,
    )(*arrays)


def rms_scale(v):
    return lax.rsqrt(jnp.mean(v * v, axis=-1, keepdims=True) + EPSILON)


def norm_reverse(v, scale, gain, grad):
    weighted = grad * gain
    return scale * weighted - v * scale * scale * scale * jnp.mean(weighted * v, axis=-1, keepdims=True)


def dot(a, b):
    return jnp.dot(a, b, preferred_element_type=F32)


def contract_rows(left, right):
    return lax.dot_general(left, right, (((0,), (0,)), ((), ())), preferred_element_type=F32)


def back_project(grad, weight):
    return lax.dot_general(grad, weight, (((1,), (1,)), ((), ())), preferred_element_type=F32)


def on_device(
    tokens, norm_gain, in_weight, conv_weight, out_weight, ffn_gain, gate_weight, up_weight, down_weight, cotangent
):
    member = lax.axis_index("replica") % 8
    lanes = member * 128

    w_in_own = jnp.concatenate(
        [lax.dynamic_slice_in_dim(in_weight, part * D + lanes, 128, axis=1) for part in range(3)], axis=1
    )
    column = lax.broadcasted_iota(jnp.int32, (8 * 576, FS), 0)
    place = lax.broadcasted_iota(jnp.int32, (8 * 576, FS), 1)
    chosen = (place % PAD < SEG) & (column == (place // PAD) * 576 + member * SEG + place % PAD)
    pick = chosen.astype(BF)
    gate_own = dot(gate_weight, pick).astype(BF)
    up_own = dot(up_weight, pick).astype(BF)
    down_own = jnp.pad(lax.dynamic_slice_in_dim(down_weight, member * SEG, SEG, axis=0), ((0, PAD - SEG), (0, 0)))
    small_own = jnp.concatenate([norm_gain[None], ffn_gain[None], conv_weight, jnp.zeros((11, 128), BF)], axis=0)

    tok, w_in, w_out, small = gather([tokens], [w_in_own, out_weight, small_own], 0, "gather_tokens")
    w_in = w_in.reshape(D, 384)
    w_out = w_out.reshape(D, D)
    small = small.transpose(1, 0, 2).reshape(16, D).astype(F32)
    gain_one, gain_two = small[0], small[1]
    taps = lax.dynamic_slice_in_dim(small[2:5], lanes, 128, axis=1)

    h0 = tok.reshape(T, D).astype(F32)
    s1 = rms_scale(h0)
    n1 = (h0 * s1 * gain_one).astype(BF)
    p = dot(n1, w_in)
    b_part, c_part, x_part = p[:, :128], p[:, 128:256], p[:, 256:]
    u = b_part * x_part
    up2 = jnp.concatenate([jnp.zeros((2, 128), F32), u], axis=0)
    v = taps[0] * up2[:T] + taps[1] * up2[1 : T + 1] + taps[2] * up2[2:]
    z_own = (c_part * v).astype(BF)

    z, e, w_gate, w_up, w_down = gather(
        [z_own, cotangent], [gate_own, up_own, down_own], 1, "gather_z"
    )
    w_gate, w_up, w_down = w_gate.reshape(D, FS), w_up.reshape(D, FS), w_down.reshape(FS, D)
    e = e.reshape(T, D)

    h1 = h0 + dot(z, w_out)
    s2 = rms_scale(h1)
    n2 = (h1 * s2 * gain_two).astype(BF)
    g = dot(n2, w_gate)
    q = dot(n2, w_up)
    sig = jax.nn.sigmoid(g)
    act = g * sig
    a = (act * q).astype(BF)
    out_share = dot(a, w_down).astype(BF)
    da = back_project(e, w_down)
    dg = (da * q * sig * (1.0 + g * (1.0 - sig))).astype(BF)
    dq = (da * act).astype(BF)
    dn2_share = back_project(dg, w_gate) + back_project(dq, w_up)
    d_gain_two = jnp.sum(dn2_share * h1 * s2, axis=0)
    out_sum, dn2 = team_sum(
        [out_share.reshape(TEAM, ROWS, D), dn2_share.astype(BF).reshape(TEAM, ROWS, D)], 2, "sum_ffn"
    )
    d_gate = contract_rows(n2, dg).astype(BF)
    d_up = contract_rows(n2, dq).astype(BF)
    d_down = contract_rows(a, e).astype(BF)

    h0_own = tokens.astype(F32)
    h1_own = lax.dynamic_slice_in_dim(h1, member * ROWS, ROWS, axis=0)
    s2_own = rms_scale(h1_own)
    block_out = (h1_own + out_sum).astype(BF)
    dh1 = cotangent.astype(F32) + norm_reverse(h1_own, s2_own, gain_two, dn2)
    (do,) = gather([dh1.astype(BF)], [], 3, "gather_do")
    do = do.reshape(T, D)

    d_out = contract_rows(z, lax.dynamic_slice_in_dim(do, lanes, 128, axis=1)).astype(BF)
    dz = back_project(do, lax.dynamic_slice_in_dim(w_out, lanes, 128, axis=0))
    dc = dz * v
    dv = dz * c_part
    d_conv = jnp.stack([jnp.sum(dv * up2[k : T + k], axis=0) for k in range(3)], axis=0)
    after = jnp.concatenate([dv, jnp.zeros((2, 128), F32)], axis=0)
    du = taps[0] * after[2:] + taps[1] * after[1 : T + 1] + taps[2] * after[:T]
    dp = jnp.concatenate([du * x_part, dc, du * b_part], axis=1).astype(BF)
    d_in = contract_rows(n1, dp).astype(BF)
    dn1_share = back_project(dp, w_in)
    d_gain_one = jnp.sum(dn1_share * h0 * s1, axis=0)
    (dn1,) = team_sum([dn1_share.astype(BF).reshape(TEAM, ROWS, D)], 4, "sum_dn1")
    token_grad = dh1 + norm_reverse(h0_own, rms_scale(h0_own), gain_one, dn1)

    d_conv = lax.dynamic_update_slice(jnp.zeros((3, D), F32), d_conv, (0, lanes))
    d_small = jnp.concatenate([d_gain_one[None], d_gain_two[None], d_conv, jnp.zeros((3, D), F32)], axis=0)
    d_small = d_small.reshape(8, 8, 128).transpose(1, 0, 2)
    s_gate, s_up, s_down, s_in, s_out, s_small = grad_sum(
        [
            d_gate.reshape(8, 128, FS),
            d_up.reshape(8, 128, FS),
            d_down.reshape(8, PAD, D),
            d_in.reshape(8, 128, 384),
            d_out.reshape(8, 128, 128),
            d_small,
        ],
        5,
        "sum_grads",
    )

    def columns(s):
        s = s.reshape(8, 128, 8, PAD)[..., :SEG]
        return s.transpose(1, 2, 0, 3).reshape(128, 8 * 576).astype(F32)

    g_in = s_in.reshape(8, 128, 3, 128).transpose(1, 2, 0, 3).reshape(128, 3 * D).astype(F32)
    g_out = s_out.transpose(1, 0, 2).reshape(128, D).astype(F32)
    g_down = s_down[:, :SEG].reshape(576, D).astype(F32)
    g_small = jnp.sum(s_small, axis=0)
    return (
        block_out,
        token_grad,
        g_small[0],
        g_in,
        g_small[2:5],
        g_out,
        g_small[1],
        columns(s_gate),
        columns(s_up),
        g_down,
    )


def solution(mesh):
    tok = P(("group", "replica"), None)
    rows = P("group", None)
    in_specs = (tok, P("group"), rows, P(None, "group"), rows, P("group"), rows, rows, rows, tok)
    out_specs = (tok, tok, P("group"), rows, P(None, "group"), rows, P("group"), rows, rows, rows)
    return jax.shard_map(on_device, mesh=mesh, in_specs=in_specs, out_specs=out_specs, check_vma=False)
```

time: 2010 us -> 466 us (0.23)
  waiting for transfers between devices: 1230 us -> 0 us
  blocking collectives: 575 us -> 0 us
  Pallas kernels: 0 us -> 324 us
  starting transfers between devices: 40 us -> 0 us
    reduce_scatter x4 -> x0, waiting for transfers between devices: 760 us -> none  [the longest x1 544 us: on_device(): lax.psum_scatter(grad_terms[3], ('group', 'replica'), scatter_dimension=0...]
    all_gather x8 -> x0, waiting for transfers between devices: 462 us -> none  [the longest x1 118 us: on_device(): lax.all_gather(gate_weight, 'group', axis=0, tiled=True)]
    unnamed x3 -> x0, blocking collectives: 462 us -> none
    pallas_call x0 -> x6, Pallas kernels: none -> 324 us  [the longest x3 135 us: gather(): pl.pallas_call(functools.partial(gather_kernel, len(team), len(group)), o...]
    all_gather x6 -> x0, blocking collectives: 114 us -> none  [the longest x1 24.2 us: on_device(): lax.all_gather(shares[3].astype(jnp.bfloat16), 'replica', axis=0, tiled=T...]
    unnamed x13 -> x0, starting transfers between devices: 33.1 us -> none
    dot_general x10 -> x12, matrix products: 64.2 us -> 62.1 us  [the longest x7 33.8 us: dot(): return jnp.dot(a, b, preferred_element_type=F32)]
  transfers between devices with their start and end apart: 27 -> 0, of which waited for: 14 -> 0; matrix products, arithmetic and copies ran while one was open for 24% -> 0% of each run, Pallas kernels for 0% -> 0%
where the time goes in v1:
time: 466 us; the launch traced here: 460 us
  Pallas kernels  324 us (70%)
  matrix products  86.5 us (19%)
  local copies, waits for them, and re-layouts  24.4 us (5%)
  other arithmetic  23.8 us (5%)
    pallas_call x3, Pallas kernels, gather(): pl.pallas_call(functools.partial(gather_kernel, len(team), len(group)), o...  135 us
    pallas_call x1, Pallas kernels, grad_sum(): pl.pallas_call(functools.partial(grad_sum_kernel, n), out_shape=[jax.Shap...  101 us
    pallas_call x2, Pallas kernels, team_sum(): pl.pallas_call(functools.partial(team_sum_kernel, n), out_shape=[jax.Shap...  88.3 us
    dot_general x7, matrix products, dot(): return jnp.dot(a, b, preferred_element_type=F32)  33.8 us
    dot_general x5, matrix products, back_project(): lax.dot_general(grad, weight, (((1,), (1,)), ((), ())), preferred_element...  28.3 us
    dot_general x5, matrix products, contract_rows(): lax.dot_general(left, right, (((0,), (0,)), ((), ())), preferred_element_...  24.5 us
    unnamed x49, local copies, waits for them, and re-layouts  12.7 us

profile of v1, /device:TPU:1, one launch (start us, length us, event | category | flops | bytes accessed | tf_op | source)
XLA Modules:
  0.0 460.1 jit_solution(8918006613505947977)
XLA Ops:
  5.4 3.5 fusion.11.refs_3_
  8.9 3.4 fusion.10.refs_2_
  12.3 46.6 %gather_tokens.1 = (bf16[8,256,1024]{2,1,0:T(8,128)(2,1)}, bf16[8,128,384]{2,1,0:T(8,128)(2,1)}, bf16[8,128,1024]{2,1,0:T(8,128)(2,1)}, bf16[8,16,128]{2,1,0:T(8,128)(2,1)}) custom-call(bf16[256,1024]{1,0:T(8,128)(2,1)} %refs_0_.1, bf16[128,384]{1,0:T(8,128)(2,1)} %pad_maximum_fusion.3.refs_1_, bf16[128,1024]{1,0:T(8,128)(2,1)} %refs_2_.1, ...), custom_call_target="tpu_custom_call" | custom-call | tf_op jit(solution)/shard_map/gather_tokens/pallas_call | solution.py:181
  59.0 3.2 fusion.2
  69.3 57.5 %gather_z.1 = (bf16[2048,1024]{1,0:T(8,128)(2,1)}, bf16[8,256,1024]{2,1,0:T(8,128)(2,1)}, bf16[8,128,640]{2,1,0:T(8,128)(2,1)}, bf16[8,128,640]{2,1,0:T(8,128)(2,1)}, bf16[8,80,1024]{2,1,0:T(8,128)(2,1)}) custom-call(bf16[2048,128]{1,0:T(8,128)(2,1)} %get-tuple-element.76.refs_0_, bf16[256,1024]{1,0:T(8,128)(2,1)} %refs_1_.1, ...), custom_call_target="tpu_custom_call" | custom-call | tf_op jit(solution)/shard_map/gather_z/pallas_call | solution.py:181
  126.8 9.2 %multiply_reduce_fusion.1 = (f32[2048]{0:T(1024)S(1)}, f32[2048,1024]{1,0:T(8,128)S(1)}) fusion(bf16[2048,1024]{1,0:T(8,128)(2,1)} %get-tuple-element.30, bf16[1024,1024]{1,0:T(8,128)(2,1)} %bitcast.135, bf16[8,256,1024]{2,1,0:T(8,128)(2,1)} %get-tuple-element.27), kind=kOutput, calls=%fused_computation.18 | convolution fusion | flops 4303353856 | bytes 18882560 | tf_op jit(solution)/shard_map/dot_general | solution.py:331
  138.4 5.0 %fusion.40 = f32[2048,640]{1,0:T(8,128)} fusion(bf16[2048,1024]{1,0:T(8,128)(2,1)S(1)} %multiply_convert_fusion, bf16[1024,640]{1,0:T(8,128)(2,1)S(1)} %bitcast.121), kind=kOutput, calls=%fused_computation.112 | convolution fusion | flops 2684354560 | bytes 10747904 | tf_op jit(solution)/shard_map/dot_general | solution.py:331
  143.4 5.1 %fusion.39 = f32[2048,640]{1,0:T(8,128)} fusion(bf16[2048,1024]{1,0:T(8,128)(2,1)S(1)} %multiply_convert_fusion, bf16[1024,640]{1,0:T(8,128)(2,1)S(1)} %bitcast.147), kind=kOutput, calls=%fused_computation.111 | convolution fusion | flops 2684354560 | bytes 10747904 | tf_op jit(solution)/shard_map/dot_general | solution.py:331
  148.5 9.0 %multiply_convert_fusion.1 = (bf16[2048,640]{1,0:T(8,128)(2,1)S(1)}, bf16[2048,640]{1,0:T(8,128)(2,1)S(1)}, bf16[2048,640]{1,0:T(8,128)(2,1)}) fusion(f32[2048,640]{1,0:T(8,128)} %fusion.39, f32[2048,640]{1,0:T(8,128)} %fusion.40, bf16[2048,1024]{1,0:T(8,128)(2,1)S(1)} %bitcast.145, bf16[640,1024]{1,0:T(8,128)(2,1)S(1)} %bitcast.149), kind=kOutput, calls=%fused_computation.19 | convolution fusion | flops 2704015360 | bytes 23855104 | tf_op jit(solution)/shard_map/dot_general | solution.py:339
  157.4 7.6 %convolution_convert_fusion.1 = bf16[640,1024]{1,0:T(8,128)(2,1)} fusion(bf16[2048,640]{1,0:T(8,128)(2,1)} %get-tuple-element.80, bf16[2048,1024]{1,0:T(8,128)(2,1)S(1)} %bitcast.146), kind=kOutput, calls=%fused_computation.28 | convolution fusion | flops 2685009920 | bytes 8126464 | tf_op jit(solution)/shard_map/dot_general | solution.py:335
  165.1 4.5 convolution_convert_fusion.2
  169.6 4.6 convolution_convert_fusion.3
  174.2 5.2 %convolution_convert_fusion = bf16[2048,1024]{1,0:T(8,128)(2,1)} fusion(bf16[2048,640]{1,0:T(8,128)(2,1)S(1)} %copy-done.21, bf16[640,1024]{1,0:T(8,128)(2,1)S(1)} %bitcast.150), kind=kOutput, calls=%fused_computation.25 | convolution fusion | flops 2686451712 | bytes 8126464 | tf_op jit(solution)/shard_map/dot_general | solution.py:331
  179.4 3.5 fusion.41
  182.9 8.5 %multiply_reduce_fusion = (f32[1024]{0:T(1024)S(1)}, bf16[2048,1024]{1,0:T(8,128)(2,1)}) fusion(f32[2048,1024]{1,0:T(8,128)S(1)} %get-tuple-element.101, f32[2048]{0:T(1024)S(1)} %add_rsqrt_fusion, f32[2048,1024]{1,0:T(8,128)S(1)} %fusion.41, bf16[2048,640]{1,0:T(8,128)(2,1)} %copy-done.9, bf16[1024,640]{1,0:T(8,128)(2,1)} %bitcast.120), kind=kOutput, calls=%fused_computation.16 | convolution fusion | flops 2694839296 | bytes 24915968 | tf_op jit(solution)/shard_map/dot_general | solution.py:339
  191.4 56.1 %sum_ffn.1 = (f32[256,1024]{1,0:T(8,128)}, f32[256,1024]{1,0:T(8,128)}) custom-call(bf16[8,256,1024]{2,1,0:T(8,128)(2,1)} %bitcast.117, bf16[8,256,1024]{2,1,0:T(8,128)(2,1)} %bitcast.109), custom_call_target="tpu_custom_call" | custom-call | tf_op jit(solution)/shard_map/sum_ffn/pallas_call | solution.py:240
  249.4 3.4 fusion.36
  252.8 30.6 %gather_do.1 = bf16[8,256,1024]{2,1,0:T(8,128)(2,1)} custom-call(bf16[256,1024]{1,0:T(8,128)(2,1)} %get-tuple-element.74.refs_0_), custom_call_target="tpu_custom_call" | custom-call | tf_op jit(solution)/shard_map/gather_do/pallas_call | solution.py:181
  283.4 4.5 convolution_convert_fusion.5
  293.3 4.3 fusion.8
  297.7 3.2 convolution_convert_fusion.4
  300.9 32.2 %sum_dn1.1 = f32[256,1024]{1,0:T(8,128)} custom-call(bf16[8,256,1024]{2,1,0:T(8,128)(2,1)} %bitcast.116), custom_call_target="tpu_custom_call" | custom-call | tf_op jit(solution)/shard_map/sum_dn1/pallas_call | solution.py:240
  337.9 100.7 %sum_grads.1 = (bf16[8,128,640]{2,1,0:T(8,128)(2,1)}, bf16[8,128,640]{2,1,0:T(8,128)(2,1)}, bf16[8,80,1024]{2,1,0:T(8,128)(2,1)}, bf16[8,128,384]{2,1,0:T(8,128)...) custom-call(bf16[8,128,640]{2,1,0:T(8,128)(2,1)} %bitcast.124, bf16[8,128,640]{2,1,0:T(8,128)(2,1)} %bitcast.123, ...), custom_call_target="tpu_custom_call" | custom-call | tf_op jit(solution)/shard_map/sum_grads/pallas_call | solution.py:297
  456.6 3.0 copy.48
  (100 shorter events, 44.0 us)
Async XLA Ops:
  0.6 4.8 %copy-start = (bf16[128,4608]{1,0:T(8,128)(2,1)S(1)}, bf16[128,4608]{1,0:T(8,128)(2,1)}, u32[]{:S(2)}) copy-start(bf16[128,4608]{1,0:T(8,128)(2,1)} %param.17) | copy-start | bytes 3538948
  5.4 3.5 copy-start.16
  59.0 3.3 copy-start.11
  59.0 3.5 copy-start.4
  62.4 1.6 copy-start.17
  66.4 1.7 copy-start.6
  136.0 46.9 %copy-start.2 = (f32[2048,1024]{1,0:T(8,128)}, f32[2048,1024]{1,0:T(8,128)S(1)}, u32[]{:S(2)}) copy-start(f32[2048,1024]{1,0:T(8,128)S(1)} %get-tuple-element.101) | copy-start | bytes 25165828
  136.0 2.3 copy-start.10
  138.4 5.0 %copy-start.13 = (bf16[8,128,640]{2,1,0:T(8,128)(2,1)S(1)}, bf16[8,128,640]{2,1,0:T(8,128)(2,1)}, u32[]{:S(2)}) copy-start(bf16[8,128,640]{2,1,0:T(8,128)(2,1)} %get-tuple-element.32) | copy-start | bytes 3932164
  143.4 5.1 %copy-start.12 = (bf16[8,256,1024]{2,1,0:T(8,128)(2,1)S(1)}, bf16[8,256,1024]{2,1,0:T(8,128)(2,1)}, u32[]{:S(2)}) copy-start(bf16[8,256,1024]{2,1,0:T(8,128)(2,1)} %get-tuple-element.35) | copy-start | bytes 12582916
  143.4 5.1 %copy-start.15 = (bf16[8,80,1024]{2,1,0:T(8,128)(2,1)S(1)}, bf16[8,80,1024]{2,1,0:T(8,128)(2,1)}, u32[]{:S(2)}) copy-start(bf16[8,80,1024]{2,1,0:T(8,128)(2,1)} %get-tuple-element.34) | copy-start | bytes 3932164
  157.4 7.6 %copy-start.9 = (bf16[2048,640]{1,0:T(8,128)(2,1)}, bf16[2048,640]{1,0:T(8,128)(2,1)S(1)}, u32[]{:S(2)}) copy-start(bf16[2048,640]{1,0:T(8,128)(2,1)S(1)} %get-tuple-element.78) | copy-start | bytes 7864324
  157.4 12.2 %copy-start.19 = (bf16[2048,640]{1,0:T(8,128)(2,1)}, bf16[2048,640]{1,0:T(8,128)(2,1)S(1)}, u32[]{:S(2)}) copy-start(bf16[2048,640]{1,0:T(8,128)(2,1)S(1)} %get-tuple-element.79) | copy-start | bytes 7864324
  169.6 4.6 copy-start.21
  174.2 5.2 %copy-start.14 = (bf16[8,128,640]{2,1,0:T(8,128)(2,1)S(1)}, bf16[8,128,640]{2,1,0:T(8,128)(2,1)}, u32[]{:S(2)}) copy-start(bf16[8,128,640]{2,1,0:T(8,128)(2,1)} %get-tuple-element.32) | copy-start | bytes 3932164
  174.2 5.2 %copy-start.20 = (bf16[2048,640]{1,0:T(8,128)(2,1)S(1)}, bf16[2048,640]{1,0:T(8,128)(2,1)}, u32[]{:S(2)}) copy-start(bf16[2048,640]{1,0:T(8,128)(2,1)} %copy-done.19) | copy-start | bytes 7864324
  283.4 4.5 copy-start.3
  287.9 3.1 copy-start.7
  290.9 2.2 copy-start.5
  290.9 2.4 copy-start.18
  300.9 32.2 %copy-start.8 = (bf16[256,1024]{1,0:T(8,128)(2,1)S(1)}, bf16[256,1024]{1,0:T(8,128)(2,1)}, u32[]{:S(2)}) copy-start(bf16[256,1024]{1,0:T(8,128)(2,1)} %refs_0_.1) | copy-start | bytes 1572868
  452.0 7.7 %copy-start.1 = (bf16[128,4608]{1,0:T(8,128)(2,1)S(1)}, bf16[128,4608]{1,0:T(8,128)(2,1)}, u32[]{:S(2)}) copy-start(bf16[128,4608]{1,0:T(8,128)(2,1)} %param.17) | copy-start | bytes 3538948

commit v2 on v1

v2 whole, which is shorter than its diff:
```python
import functools

import jax
import jax.numpy as jnp
from jax import lax
from jax.experimental import pallas as pl
from jax.experimental.pallas import tpu as pltpu
from jax.sharding import PartitionSpec as P

MESH = pl.DeviceIdType.MESH
EPSILON = 1e-06
BF = jnp.bfloat16
F32 = jnp.float32
D = 1024
SEG = 72
PAD = 80
FS = 8 * PAD
TEAM = 8
ROWS = 256
T = TEAM * ROWS
VLIM = 60 * 2**20


def coords():
    group, replica = lax.axis_index("group"), lax.axis_index("replica")
    return group // 2, group % 2, replica // 8, (replica // 2) % 4, replica % 2


def device(x, zh, zl, y, c):
    return (x * 2 + zh, zl * 8 + y * 2 + c)


def remote(src, dst, send, recv, target):
    return pltpu.make_async_remote_copy(
        src_ref=src, dst_ref=dst, send_sem=send, recv_sem=recv, device_id=target, device_id_type=MESH
    )


def team_peers():
    x, zh, zl, y, c = coords()
    return [device(x, zh, zl, y, 1 - c)] + [device(x, zh, zl, (y + d) % 4, c) for d in (1, 2, 3)]


def group_peers():
    x, zh, zl, y, c = coords()
    return [
        device((x + dx) % 4, (zh + dz) % 2, zl, y, c)
        for dx in range(4)
        for dz in range(2)
        if (dx, dz) != (0, 0)
    ]


def z_peer():
    x, zh, zl, y, c = coords()
    return device(x, zh, 1 - zl, y, c)


def meet(peers):
    barrier = pltpu.get_barrier_semaphore()
    for peer in peers:
        pl.semaphore_signal(barrier, inc=1, device_id=peer, device_id_type=MESH)
    pl.semaphore_wait(barrier, len(peers))


class TeamGather:
    def __init__(self, src, part, send, recv, local):
        x, zh, zl, y, c = coords()
        sibling = device(x, zh, zl, y, 1 - c)
        right, left = device(x, zh, zl, (y + 1) % 4, c), device(x, zh, zl, (y + 3) % 4, c)
        me = 2 * y + c
        before, after, across = 2 * ((y + 3) % 4) + c, 2 * ((y + 1) % 4) + c, 2 * ((y + 2) % 4) + c
        self.own = pltpu.make_async_copy(src, part(me, None), local)

        def hop(source, block, half, k, target):
            return remote(source, part(block, half), send.at[k], recv.at[k], target)

        self.pair = hop(src, me, None, 0, sibling)
        self.out = [hop(src, me, None, 1, right), hop(src, me, None, 2, left)]
        self.near = [hop(src, before, None, 1, right), hop(src, after, None, 2, left)]
        self.onward = [
            hop(part(before, 0), before, 0, 3, right),
            hop(part(after, 1), after, 1, 4, left),
        ]
        self.far = [
            hop(part(across, 0), across, 0, 3, right),
            hop(part(across, 1), across, 1, 4, left),
        ]
        self.handed = [
            hop(part(before, None), before, None, 5, sibling),
            hop(part(after, None), after, None, 6, sibling),
            hop(part(across, 0), across, 0, 7, sibling),
            hop(part(across, 1), across, 1, 8, sibling),
        ]

    def start(self):
        for copy in self.out:
            copy.start()
        self.pair.start()
        self.own.start()

    def step(self):
        for i in range(2):
            self.near[i].wait_recv()
            self.onward[i].start()
            self.handed[i].start()

    def finish(self):
        for i in range(2):
            self.far[i].wait_recv()
            self.handed[2 + i].start()
        self.own.wait()
        self.pair.wait()
        for copy in self.out + self.onward:
            copy.wait_send()
        for copy in self.handed:
            copy.wait()


def block_part(ref):
    rows = ref.shape[1]
    unit = 8 if ref.dtype == F32 else 16
    cut = (rows // 2 + unit - 1) // unit * unit

    def part(i, half):
        if half is None:
            return ref.at[i]
        return ref.at[i, pl.ds(0, cut)] if half == 0 else ref.at[i, pl.ds(cut, rows - cut)]

    return part


def lane_part(ref):
    rows = ref.shape[0]

    def part(i, half):
        lanes = pl.ds(pl.multiple_of(i * 128, 128), 128)
        if half is None:
            return ref.at[:, lanes]
        return ref.at[pl.ds(half * (rows // 2), rows // 2), lanes]

    return part


class GroupGather:
    def __init__(self, src, slot, send, recv, local):
        x, zh, zl, y, c = coords()
        right, left = device((x + 1) % 4, zh, zl, y, c), device((x + 3) % 4, zh, zl, y, c)
        me, partner = 2 * x + zh, 2 * x + 1 - zh
        before, after, across = 2 * ((x + 3) % 4), 2 * ((x + 1) % 4), 2 * ((x + 2) % 4)
        self.own = pltpu.make_async_copy(src, slot(me), local)

        def hop(source, block, k, target):
            return remote(source, slot(block), send.at[k], recv.at[k], target)

        self.pair = hop(src, me, 0, device(x, 1 - zh, zl, y, c))
        self.out = [hop(src, me, 1, right), hop(src, me, 2, left)]
        self.paired = hop(src, partner, 0, right)
        self.second = [hop(slot(partner), partner, 3, right), hop(slot(partner), partner, 4, left)]
        self.first_in = [hop(src, before, 1 + 2 * zh, right), hop(src, after + 1, 4 - 2 * zh, left)]
        self.onward = [hop(slot(before), before, 5, right), hop(slot(after + 1), after + 1, 6, left)]
        self.last_in = [
            hop(src, before + 1, 3 - 2 * zh, right),
            hop(src, after, 2 + 2 * zh, left),
            hop(src, across, 5, right),
            hop(src, across + 1, 6, left),
        ]

    def start(self):
        self.pair.start()
        for copy in self.out:
            copy.start()
        self.own.start()

    def step(self):
        self.paired.wait_recv()
        for copy in self.second:
            copy.start()

    def relay(self):
        for i in range(2):
            self.first_in[i].wait_recv()
            self.onward[i].start()

    def finish(self):
        self.own.wait()
        for copy in self.last_in:
            copy.wait_recv()
        for copy in [self.pair] + self.out + self.second + self.onward:
            copy.wait_send()


class GroupSum:
    def __init__(self, share, out, half_land, land, z_land, stage, send, recv, tsend, trecv, local):
        x, zh, zl, y, c = coords()
        self.share, self.half_land, self.land, self.z_land, self.stage = share, half_land, land, z_land, stage
        right, left = device((x + 1) % 4, zh, zl, y, c), device((x + 3) % 4, zh, zl, y, c)
        far, self.near, self.back = 2 * ((x + 2) % 4), 2 * ((x + 1) % 4), 2 * ((x + 3) % 4)
        self.here, self.zh = 2 * x, zh
        moves = [
            (share.at[far], half_land.at[0], right),
            (share.at[far + 1], half_land.at[1], left),
            (share.at[pl.ds(self.near, 2)], land.at[0], right),
            (share.at[pl.ds(self.back, 2)], land.at[1], left),
            (stage.at[0], z_land.at[0], device(x, 1 - zh, zl, y, c)),
            (stage.at[1], z_land.at[1], device(x, zh, 1 - zl, y, c)),
        ]
        self.hops = [remote(src, dst, send.at[k], recv.at[k], to) for k, (src, dst, to) in enumerate(moves)]
        self.gather = TeamGather(stage.at[2], block_part(out), tsend, trecv, local)

    def far_out(self):
        self.hops[0].start()
        self.hops[1].start()

    def near_out(self):
        share, kind = self.share, self.share.dtype
        self.hops[0].wait_recv()
        share[self.near] = (share[self.near].astype(F32) + self.half_land[0].astype(F32)).astype(kind)
        self.hops[2].start()
        self.hops[1].wait_recv()
        share[self.back + 1] = (share[self.back + 1].astype(F32) + self.half_land[1].astype(F32)).astype(kind)
        self.hops[3].start()

    def ring_total(self, k):
        return self.share[self.here + k].astype(F32) + self.land[0, k].astype(F32) + self.land[1, k].astype(F32)

    def z_out(self):
        self.hops[2].wait_recv()
        self.hops[3].wait_recv()
        self.stage[0] = self.ring_total(1 - self.zh).astype(self.stage.dtype)
        self.hops[4].start()

    def z_lo_out(self):
        own = self.ring_total(self.zh)
        self.hops[4].wait()
        self.stage[1] = (own + self.z_land[0].astype(F32)).astype(self.stage.dtype)
        self.hops[5].start()

    def team_out(self):
        self.hops[5].wait()
        self.stage[2] = (self.stage[1].astype(F32) + self.z_land[1].astype(F32)).astype(self.stage.dtype)
        self.gather.start()

    def finish(self):
        self.gather.finish()
        for k in range(4):
            self.hops[k].wait_send()

    @staticmethod
    def scratch(r, w, kind):
        return [
            pltpu.VMEM((2, r, w), kind),
            pltpu.VMEM((2, 2, r, w), kind),
            pltpu.VMEM((2, r, w), kind),
            pltpu.VMEM((3, r, w), kind),
            pltpu.SemaphoreType.DMA((6,)),
            pltpu.SemaphoreType.DMA((6,)),
            pltpu.SemaphoreType.DMA((9,)),
            pltpu.SemaphoreType.DMA((9,)),
            pltpu.SemaphoreType.DMA(()),
        ]


def pick(i, values):
    out = values[-1]
    for k in range(len(values) - 2, -1, -1):
        out = jnp.where(i == k, values[k], out)
    return out


def front_kernel(
    tokens, cotangent, small_own, in_own, out_own, gu_own, down_own,
    tok, e, w_in, w_out, w_gu, w_down, gains, p, v, z,
    small, z_own, tsend, trecv, gsend, grecv, local, hsend, hrecv,
):
    x, zh, zl, y, c = coords()
    member = 2 * y + c
    meet(team_peers() + x_peers() + [device(x, 1 - zh, zl, y, c)])
    tok_job = TeamGather(tokens, block_part(tok), tsend.at[0], trecv.at[0], local.at[0])
    e_job = TeamGather(cotangent, block_part(e), tsend.at[1], trecv.at[1], local.at[1])
    z_job = TeamGather(z_own, lane_part(z), tsend.at[2], trecv.at[2], local.at[2])
    out_rows = pl.ds(pl.multiple_of(c * 64, 64), 64)
    slots = [
        lambda k: small.at[k],
        lambda k: w_in.at[pl.ds(pl.multiple_of(k * 128, 128), 128)],
        lambda k: w_out.at[k, out_rows],
        lambda k: w_gu.at[pl.ds(pl.multiple_of(k * 128, 128), 128)],
        lambda k: w_down.at[pl.ds(pl.multiple_of(k * PAD, PAD), PAD)],
    ]
    owned = [small_own, in_own, out_own.at[out_rows], gu_own, down_own]
    jobs = [
        GroupGather(src, slot, gsend.at[i], grecv.at[i], local.at[3 + i])
        for i, (src, slot) in enumerate(zip(owned, slots))
    ]
    tok_job.start()
    for job in jobs:
        job.start()
    tok_job.step()
    e_job.start()
    for job in jobs[:3]:
        job.step()
    jobs[0].relay()
    jobs[1].relay()
    tok_job.finish()
    jobs[0].finish()
    jobs[1].finish()
    for job in jobs[3:]:
        job.step()
    jobs[2].relay()
    for g in range(8):
        gains[:, 128 * g : 128 * g + 128] = small[g].astype(F32)
    taps = gains[:, pl.ds(pl.multiple_of(member * 128, 128), 128)]

    def project(b, last):
        rows = pl.ds(pl.multiple_of(b * ROWS, ROWS), ROWS)
        h0 = tok[b].astype(F32)
        n1 = (h0 * rms_scale(h0) * gains[0:1]).astype(BF)
        block = dot(n1, w_in[...])
        p[rows] = block
        mixed = block[:, :128] * block[:, 256:]
        behind = jnp.concatenate([last, mixed], axis=0)
        conv = taps[2:3] * behind[6 : ROWS + 6] + taps[3:4] * behind[7 : ROWS + 7] + taps[4:5] * behind[8:]
        v[rows] = conv
        z_own[rows] = (block[:, 128:256] * conv).astype(BF)
        return mixed[ROWS - 8 :]

    lax.fori_loop(0, 8, project, jnp.zeros((8, 128), F32))
    z_job.start()
    e_job.step()
    jobs[3].relay()
    jobs[4].relay()
    jobs[2].finish()
    handed = remote(w_out.at[:, out_rows], w_out.at[:, out_rows], hsend, hrecv, device(x, zh, zl, y, 1 - c))
    handed.start()
    e_job.finish()
    z_job.step()
    z_job.finish()
    other_rows = pl.ds(pl.multiple_of(64 - c * 64, 64), 64)
    jobs[3].finish()
    jobs[4].finish()
    handed.wait_send()
    remote(w_out.at[:, out_rows], w_out.at[:, other_rows], hsend, hrecv, device(x, zh, zl, y, 1 - c)).wait_recv()


def front(tokens, cotangent, small_own, in_own, out_own, gu_own, down_own, collective_id, name):
    vmem, anywhere = pl.BlockSpec(memory_space=pltpu.VMEM), pl.BlockSpec(memory_space=pl.ANY)
    shape = jax.ShapeDtypeStruct
    return pl.pallas_call(
        front_kernel,
        out_shape=[
            shape((TEAM, ROWS, D), BF),
            shape((TEAM, ROWS, D), BF),
            shape((D, 384), BF),
            shape((8, 128, D), BF),
            shape((D, 2 * FS), BF),
            shape((FS, D), BF),
            shape((16, D), F32),
            shape((T, 384), F32),
            shape((T, 128), F32),
            shape((T, D), BF),
        ],
        in_specs=[anywhere] * 7,
        out_specs=[vmem, anywhere, vmem, anywhere, anywhere, anywhere, vmem, vmem, vmem, anywhere],
        scratch_shapes=[
            pltpu.VMEM((8, 16, 128), BF),
            pltpu.VMEM((T, 128), BF),
            pltpu.SemaphoreType.DMA((3, 9)),
            pltpu.SemaphoreType.DMA((3, 9)),
            pltpu.SemaphoreType.DMA((5, 7)),
            pltpu.SemaphoreType.DMA((5, 7)),
            pltpu.SemaphoreType.DMA((8,)),
            pltpu.SemaphoreType.DMA(()),
            pltpu.SemaphoreType.DMA(()),
        ],
        compiler_params=pltpu.CompilerParams(
            collective_id=collective_id, has_side_effects=True, vmem_limit_bytes=VLIM
        ),
        name=name,
    )(tokens, cotangent, small_own, in_own, out_own, gu_own, down_own)


class TeamSum:
    def __init__(self, share, pair_land, half_land, land, psend, precv, send, recv):
        x, zh, zl, y, c = coords()
        self.share, self.pair_land, self.half_land, self.land = share, pair_land, half_land, land
        sibling = device(x, zh, zl, y, 1 - c)
        right, left = device(x, zh, zl, (y + 1) % 4, c), device(x, zh, zl, (y + 3) % 4, c)
        chips = [(y + d) % 4 for d in (2, 1, 3, 0)]
        self.mine = [2 * k + c for k in chips]
        self.pairs = [
            remote(share.at[2 * chips[s] + 1 - c], pair_land.at[s], psend.at[s], precv.at[s], sibling)
            for s in range(4)
        ]
        half = ROWS // 2
        far, near, back = self.mine[0], self.mine[1], self.mine[2]
        self.hops = [
            remote(share.at[far, pl.ds(0, half)], half_land.at[0], send.at[0], recv.at[0], right),
            remote(share.at[far, pl.ds(half, half)], half_land.at[1], send.at[1], recv.at[1], left),
            remote(share.at[near], land.at[0], send.at[2], recv.at[2], right),
            remote(share.at[back], land.at[1], send.at[3], recv.at[3], left),
        ]

    def send_pair(self, s):
        self.pairs[s].start()

    def add_pair(self, s):
        share, b = self.share, self.mine[s]
        half = ROWS // 2
        self.pairs[s].wait()
        total = share[b].astype(F32) + self.pair_land[s].astype(F32)
        if s in (1, 2):
            self.hops[s - 1].wait_recv()
            rows = self.half_land[s - 1].astype(F32)
            top, low = total[:half], total[half:]
            if s == 1:
                share[b, :half] = (top + rows).astype(BF)
                share[b, half:] = low.astype(BF)
            else:
                share[b, :half] = top.astype(BF)
                share[b, half:] = (low + rows).astype(BF)
            self.hops[s + 1].start()
        else:
            share[b] = total.astype(BF)
            if s == 0:
                self.hops[0].start()
                self.hops[1].start()

    def result(self):
        for k in (0, 1):
            self.hops[k].wait_send()
        for k in (2, 3):
            self.hops[k].wait()
        b = self.mine[3]
        return self.share[b].astype(F32) + self.land[0].astype(F32) + self.land[1].astype(F32)

    @staticmethod
    def scratch(n):
        return [
            pltpu.VMEM((n, 4, ROWS, D), BF),
            pltpu.VMEM((n, 2, ROWS // 2, D), BF),
            pltpu.VMEM((n, 2, ROWS, D), BF),
            pltpu.SemaphoreType.DMA((n, 4)),
            pltpu.SemaphoreType.DMA((n, 4)),
            pltpu.SemaphoreType.DMA((n, 4)),
            pltpu.SemaphoreType.DMA((n, 4)),
        ]


def ffn_kernel(
    tok_hbm, e_hbm, z_hbm, w_out_hbm, w_gu_hbm, w_down_hbm, gain_ref,
    block_out, dh1_out, do_hbm, d_gu, d_down, gain_grad,
    tok, e, z, w_out, w_gu, w_down, n2, a, dgq, h1_ref, do_own, share, local, wlocal, blocal,
    dsend, drecv, pair_land, half_land, land, psend, precv, send, recv,
):
    x, zh, zl, y, c = coords()
    weights = [
        pltpu.make_async_copy(src, dst, wlocal.at[i])
        for i, (src, dst) in enumerate(((w_out_hbm, w_out), (w_gu_hbm, w_gu), (w_down_hbm, w_down)))
    ]
    blocks = []
    for s, turn in enumerate((2, 1, 3, 0)):
        k = (y + turn) % 4
        pair, rows = pl.ds(2 * k, 2), pl.ds(pl.multiple_of(2 * ROWS * k, 2 * ROWS), 2 * ROWS)
        blocks.append(
            [
                pltpu.make_async_copy(z_hbm.at[rows], z.at[rows], blocal.at[s, 0]),
                pltpu.make_async_copy(tok_hbm.at[pair], tok.at[pair], blocal.at[s, 1]),
                pltpu.make_async_copy(e_hbm.at[pair], e.at[pair], blocal.at[s, 2]),
            ]
        )
    weights[0].start()
    for copy in blocks[0]:
        copy.start()
    for copy in weights[1:]:
        copy.start()
    for copies in blocks[1:]:
        for copy in copies:
            copy.start()
    meet(team_peers())
    sums = [
        TeamSum(
            share.at[k], pair_land.at[k], half_land.at[k], land.at[k],
            psend.at[k], precv.at[k], send.at[k], recv.at[k],
        )
        for k in range(2)
    ]
    for copy in weights:
        copy.wait()
    gain = gain_ref[...]
    gain_grad[...] = jnp.zeros_like(gain_grad)

    def step(i, carry):
        for k in range(4):

            @pl.when(i == 2 * k)
            def _():
                for copy in blocks[k]:
                    copy.wait()

        s, own = i // 2, i % 2
        turn = jnp.where(s == 0, 2, jnp.where(s == 1, 1, jnp.where(s == 2, 3, 0)))
        b = 2 * ((y + turn) % 4) + jnp.where(own == 1, c, 1 - c)
        rows = pl.ds(pl.multiple_of(b * ROWS, ROWS), ROWS)
        h1 = tok[b].astype(F32) + dot(z[rows, :], w_out[...])
        h1_ref[...] = h1
        hs = h1 * lax.rsqrt(jnp.mean(h1 * h1, axis=-1, keepdims=True) + EPSILON)
        n2_b = (hs * gain).astype(BF)
        n2[rows, :] = n2_b
        g = dot(n2_b, w_gu[:, :FS])
        q = dot(n2_b, w_gu[:, FS:])
        sig = jax.nn.sigmoid(g)
        act = g * sig
        a_b = (act * q).astype(BF)
        a[rows, :] = a_b
        da = back_project(e[b], w_down[...])
        dgq[rows, :FS] = (da * q * sig * (1.0 + g * (1.0 - sig))).astype(BF)
        dgq[rows, FS:] = (da * act).astype(BF)
        share[1, b] = dot(a_b, w_down[...]).astype(BF)
        dn2 = back_project(dgq[rows, :], w_gu[...])
        share[0, b] = dn2.astype(BF)
        scale = lax.rsqrt(jnp.mean(h1_ref[...] * h1_ref[...], axis=-1, keepdims=True) + EPSILON)
        gain_grad[...] += jnp.sum(dn2 * (h1_ref[...] * scale), axis=0, keepdims=True)
        for k in range(4):

            @pl.when(i == 2 * k)
            def _():
                sums[0].send_pair(k)
                sums[1].send_pair(k)

            @pl.when(i == 2 * k + 1)
            def _():
                sums[0].add_pair(k)
                sums[1].add_pair(k)

        return carry

    lax.fori_loop(0, 8, step, 0)

    d_down[...] = contract_rows(a[...], e[...].reshape(T, D)).astype(BF)
    dn2 = sums[0].result()
    h1 = h1_ref[...]
    s2 = lax.rsqrt(jnp.mean(h1 * h1, axis=-1, keepdims=True) + EPSILON)
    dh1 = e[2 * y + c].astype(F32) + norm_reverse(h1, s2, gain, dn2)
    dh1_out[...] = dh1
    do_own[...] = dh1.astype(BF)
    do_job = TeamGather(do_own, block_part(do_hbm), dsend, drecv, local)
    do_job.start()

    def tile(m, carry):
        columns = pl.ds(pl.multiple_of(m * 512, 512), 512)
        d_gu[columns, :] = contract_rows(n2[:, columns], dgq[...]).astype(BF)
        return carry

    lax.fori_loop(0, 2, tile, 0)
    do_job.step()
    block_out[...] = (h1_ref[...] + sums[1].result()).astype(BF)
    do_job.finish()


def ffn(tok, e, z, w_out, w_gu, w_down, gain, collective_id, name):
    vmem, anywhere = pl.BlockSpec(memory_space=pltpu.VMEM), pl.BlockSpec(memory_space=pl.ANY)
    shape = jax.ShapeDtypeStruct
    return pl.pallas_call(
        ffn_kernel,
        out_shape=[
            shape((ROWS, D), BF),
            shape((ROWS, D), F32),
            shape((TEAM, ROWS, D), BF),
            shape((D, 2 * FS), BF),
            shape((FS, D), BF),
            shape((1, D), F32),
        ],
        in_specs=[anywhere] * 6 + [vmem],
        out_specs=[vmem, vmem, anywhere, vmem, vmem, vmem],
        scratch_shapes=[
            pltpu.VMEM((TEAM, ROWS, D), BF),
            pltpu.VMEM((TEAM, ROWS, D), BF),
            pltpu.VMEM((T, D), BF),
            pltpu.VMEM((D, D), BF),
            pltpu.VMEM((D, 2 * FS), BF),
            pltpu.VMEM((FS, D), BF),
            pltpu.VMEM((T, D), BF),
            pltpu.VMEM((T, FS), BF),
            pltpu.VMEM((T, 2 * FS), BF),
            pltpu.VMEM((ROWS, D), F32),
            pltpu.VMEM((ROWS, D), BF),
            pltpu.VMEM((2, TEAM, ROWS, D), BF),
            pltpu.SemaphoreType.DMA(()),
            pltpu.SemaphoreType.DMA((3,)),
            pltpu.SemaphoreType.DMA((4, 3)),
            pltpu.SemaphoreType.DMA((9,)),
            pltpu.SemaphoreType.DMA((9,)),
        ]
        + TeamSum.scratch(2),
        compiler_params=pltpu.CompilerParams(
            collective_id=collective_id, has_side_effects=True, vmem_limit_bytes=VLIM
        ),
        name=name,
    )(tok, e, z, w_out, w_gu, w_down, gain)


def conv_back_kernel(
    tok_hbm, do_hbm, z_hbm, d_gu_hbm, d_down_hbm, w_in, w_out_t, p, v, dh1, gains, taps,
    token_grad, gu_out, down_out, in_out, out_out, small_out,
    tok, do, z, d_gu, d_down, d_in, d_out, d_small, n1, up, dv, dp, sums, share, local, *rest,
):
    x, zh, zl, y, c = coords()
    member = 2 * y + c
    here = x * 2 + zh
    meet(team_peers() + x_peers() + [device(x, 1 - zh, zl, y, c), device(x, zh, 1 - zl, y, c)])
    loads = [
        pltpu.make_async_copy(src, dst, local.at[i])
        for i, (src, dst) in enumerate(
            ((d_gu_hbm, d_gu), (d_down_hbm, d_down), (do_hbm, do), (z_hbm, z), (tok_hbm, tok))
        )
    ]
    for copy in loads:
        copy.start()
    dn1_sum = TeamSum(share, *[ref.at[0] for ref in rest[:7]])
    parts = ((d_gu, gu_out), (d_down, down_out), (d_in, in_out), (d_out, out_out), (d_small, small_out))
    jobs = [
        GroupSum(ref, out, *rest[7 + 9 * i : 16 + 9 * i]) for i, (ref, out) in enumerate(parts)
    ]
    gu, down, in_job, out_job, small = jobs
    loads[0].wait()
    gu.far_out()
    loads[1].wait()
    down.far_out()
    loads[2].wait()

    up[pl.ds(0, 8)] = jnp.zeros((8, 128), F32)
    dv[pl.ds(T, 8)] = jnp.zeros((8, 128), F32)

    def first(b, carry):
        rows = pl.ds(pl.multiple_of(b * ROWS, ROWS), ROWS)
        dz = back_project(do[b], w_out_t[...])
        up[pl.ds(pl.multiple_of(b * ROWS, ROWS) + 8, ROWS)] = p[rows, :128] * p[rows, 256:]
        dp[rows, 128:256] = (dz * v[rows]).astype(BF)
        dv[rows] = dz * p[rows, 128:256]
        return carry

    lax.fori_loop(0, 8, first, 0)
    sums[...] = jnp.zeros_like(sums)

    def second(b, carry):
        rows = pl.ds(pl.multiple_of(b * ROWS, ROWS), ROWS)
        longer = pl.ds(pl.multiple_of(b * ROWS, ROWS), ROWS + 8)
        ahead, behind = dv[longer], up[longer]
        du = taps[0:1] * ahead[2 : ROWS + 2] + taps[1:2] * ahead[1 : ROWS + 1] + taps[2:3] * ahead[:ROWS]
        dp[rows, :128] = (du * p[rows, 256:]).astype(BF)
        dp[rows, 256:] = (du * p[rows, :128]).astype(BF)
        for k in range(3):
            sums[2 + k : 3 + k, :128] += jnp.sum(
                ahead[:ROWS] * behind[6 + k : 6 + k + ROWS], axis=0, keepdims=True
            )
        return carry

    lax.fori_loop(0, 8, second, 0)
    gu.near_out()
    down.near_out()
    loads[3].wait()
    d_out[...] = (
        contract_rows(z[...], do[:, :, pl.ds(pl.multiple_of(member * 128, 128), 128)].reshape(T, 128))
        .astype(BF)
        .reshape(8, 128, 128)
    )
    out_job.far_out()
    loads[4].wait()

    def third(i, carry):
        s, own = i // 2, i % 2
        turn = jnp.where(s == 0, 2, jnp.where(s == 1, 1, jnp.where(s == 2, 3, 0)))
        b = 2 * ((y + turn) % 4) + jnp.where(own == 1, c, 1 - c)
        rows = pl.ds(pl.multiple_of(b * ROWS, ROWS), ROWS)
        h0 = tok[b].astype(F32)
        hs = h0 * rms_scale(h0)
        n1[rows, :] = (hs * gains[0:1]).astype(BF)
        dn1 = back_project(dp[rows, :], w_in[...])
        share[b] = dn1.astype(BF)
        sums[0:1] += jnp.sum(dn1 * hs, axis=0, keepdims=True)
        for k in range(4):

            @pl.when(i == 2 * k)
            def _():
                dn1_sum.send_pair(k)

            @pl.when(i == 2 * k + 1)
            def _():
                dn1_sum.add_pair(k)

        return carry

    lax.fori_loop(0, 8, third, 0)
    d_in[...] = contract_rows(n1[...], dp[...]).astype(BF).reshape(8, 128, 384)
    in_job.far_out()
    conv = sums[2:5, :128]
    for g in range(8):
        d_small[g] = jnp.zeros((16, 128), F32)
        d_small[g, 0:1] = sums[0:1, 128 * g : 128 * g + 128]
        d_small[g, 1:2] = gains[1:2, 128 * g : 128 * g + 128]
        d_small[g, 2:5] = jnp.where(member == g, conv, 0.0)
    small.far_out()
    out_job.near_out()
    gu.z_out()
    down.z_out()
    in_job.near_out()
    small.near_out()
    out_job.z_out()
    gu.z_lo_out()
    down.z_lo_out()
    h0 = tok[member].astype(F32)
    token_grad[...] = dh1[...] + norm_reverse(h0, rms_scale(h0), gains[0:1], dn1_sum.result())
    gu.team_out()
    down.team_out()
    out_job.z_lo_out()
    in_job.z_out()
    small.z_out()
    in_job.z_lo_out()
    small.z_lo_out()
    out_job.team_out()
    in_job.team_out()
    small.team_out()
    for job in jobs:
        job.gather.step()
    for job in jobs:
        job.finish()


def x_peers():
    x, zh, zl, y, c = coords()
    return [device((x + 1) % 4, zh, zl, y, c), device((x + 3) % 4, zh, zl, y, c)]


def conv_back(tok, do, z, d_gu, d_down, w_in, w_out_t, p, v, dh1, gains, taps, collective_id, name):
    vmem, anywhere = pl.BlockSpec(memory_space=pltpu.VMEM), pl.BlockSpec(memory_space=pl.ANY)
    shape = jax.ShapeDtypeStruct
    blocks = [((128, 2 * FS), BF), ((PAD, D), BF), ((128, 384), BF), ((128, 128), BF), ((16, 128), F32)]
    scratch = [
        pltpu.VMEM((TEAM, ROWS, D), BF),
        pltpu.VMEM((TEAM, ROWS, D), BF),
        pltpu.VMEM((T, D), BF),
    ]
    scratch += [pltpu.VMEM((8,) + block, kind) for block, kind in blocks]
    scratch += [
        pltpu.VMEM((T, D), BF),
        pltpu.VMEM((T + 8, 128), F32),
        pltpu.VMEM((T + 8, 128), F32),
        pltpu.VMEM((T, 384), BF),
        pltpu.VMEM((8, D), F32),
        pltpu.VMEM((TEAM, ROWS, D), BF),
        pltpu.SemaphoreType.DMA((5,)),
    ]
    scratch += TeamSum.scratch(1)
    for block, kind in blocks:
        scratch += GroupSum.scratch(*block, kind)
    return pl.pallas_call(
        conv_back_kernel,
        out_shape=[shape((ROWS, D), F32)] + [shape((8,) + block, kind) for block, kind in blocks],
        in_specs=[anywhere] * 5 + [vmem] * 7,
        out_specs=[vmem] + [anywhere] * 5,
        scratch_shapes=scratch,
        compiler_params=pltpu.CompilerParams(
            collective_id=collective_id, has_side_effects=True, vmem_limit_bytes=VLIM
        ),
        name=name,
    )(tok, do, z, d_gu, d_down, w_in, w_out_t, p, v, dh1, gains, taps)


def rms_scale(v):
    return lax.rsqrt(jnp.mean(v * v, axis=-1, keepdims=True) + EPSILON)


def norm_reverse(v, scale, gain, grad):
    weighted = grad * gain
    return scale * weighted - v * scale * scale * scale * jnp.mean(weighted * v, axis=-1, keepdims=True)


def dot(a, b):
    return jnp.dot(a, b, preferred_element_type=F32)


def contract_rows(left, right):
    return lax.dot_general(left, right, (((0,), (0,)), ((), ())), preferred_element_type=F32)


def back_project(grad, weight):
    return lax.dot_general(grad, weight, (((1,), (1,)), ((), ())), preferred_element_type=F32)


def on_device(
    tokens, norm_gain, in_weight, conv_weight, out_weight, ffn_gain, gate_weight, up_weight, down_weight, cotangent
):
    member = lax.axis_index("replica") % 8
    lanes = member * 128

    w_in_own = jnp.concatenate(
        [lax.dynamic_slice_in_dim(in_weight, part * D + lanes, 128, axis=1) for part in range(3)], axis=1
    )
    column = lax.broadcasted_iota(jnp.int32, (8 * 576, FS), 0)
    place = lax.broadcasted_iota(jnp.int32, (8 * 576, FS), 1)
    chosen = (place % PAD < SEG) & (column == (place // PAD) * 576 + member * SEG + place % PAD)
    pick = chosen.astype(BF)
    gu_own = jnp.concatenate([dot(gate_weight, pick), dot(up_weight, pick)], axis=1).astype(BF)
    down_own = jnp.pad(lax.dynamic_slice_in_dim(down_weight, member * SEG, SEG, axis=0), ((0, PAD - SEG), (0, 0)))
    small_own = jnp.concatenate([norm_gain[None], ffn_gain[None], conv_weight, jnp.zeros((11, 128), BF)], axis=0)

    tok, e, w_in, w_out, w_gu, w_down, gains, p, v, z = front(
        tokens, cotangent, small_own, w_in_own, out_weight, gu_own, down_own, 0, "front"
    )
    w_out = w_out.reshape(D, D)
    block_out, dh1, do, d_gu, d_down, d_gain_two = ffn(tok, e, z, w_out, w_gu, w_down, gains[1:2], 1, "ffn")
    token_grad, s_gu, s_down, s_in, s_out, s_small = conv_back(
        tok,
        do,
        z,
        d_gu.reshape(8, 128, 2 * FS),
        d_down.reshape(8, PAD, D),
        w_in,
        lax.dynamic_slice_in_dim(w_out, lanes, 128, axis=0),
        p,
        v,
        dh1,
        jnp.concatenate([gains[0:1], d_gain_two, jnp.zeros((6, D), F32)], axis=0),
        jnp.pad(lax.dynamic_slice_in_dim(gains[2:5], lanes, 128, axis=1), ((0, 5), (0, 0))),
        2,
        "conv_back",
    )

    def columns(s):
        s = s.reshape(8, 128, 8, PAD)[..., :SEG]
        return s.transpose(1, 2, 0, 3).reshape(128, 8 * 576).astype(F32)

    g_in = s_in.reshape(8, 128, 3, 128).transpose(1, 2, 0, 3).reshape(128, 3 * D).astype(F32)
    g_out = s_out.transpose(1, 0, 2).reshape(128, D).astype(F32)
    g_down = s_down[:, :SEG].reshape(576, D).astype(F32)
    g_small = jnp.sum(s_small, axis=0)
    return (
        block_out,
        token_grad,
        g_small[0],
        g_in,
        g_small[2:5],
        g_out,
        g_small[1],
        columns(s_gu[..., :FS]),
        columns(s_gu[..., FS:]),
        g_down,
    )


def solution(mesh):
    tok = P(("group", "replica"), None)
    rows = P("group", None)
    in_specs = (tok, P("group"), rows, P(None, "group"), rows, P("group"), rows, rows, rows, tok)
    out_specs = (tok, tok, P("group"), rows, P(None, "group"), rows, P("group"), rows, rows, rows)
    return jax.shard_map(on_device, mesh=mesh, in_specs=in_specs, out_specs=out_specs, check_vma=False)
```

time: 466 us -> 284 us (0.61); the launches traced: 460 us -> 284 us
  matrix products: 86.5 us -> 5.54 us
  Pallas kernels: 324 us -> 246 us
  other arithmetic: 23.8 us -> 5.63 us
    pallas_call x6 -> x3, Pallas kernels: 324 us -> 246 us  [the longest x1 91.9 us: conv_back(): pl.pallas_call(conv_back_kernel, out_shape=[shape((ROWS, D), F32)] + [sha...]
    dot_general x10 -> x0, matrix products: 52.7 us -> none  [the longest x5 28.3 us: back_project(): lax.dot_general(grad, weight, (((1,), (1,)), ((), ())), preferred_element...]
    dot_general x7 -> x2, matrix products: 33.8 us -> 5.54 us  [dot(): return jnp.dot(a, b, preferred_element_type=F32)]
    slice x2 -> x5, local copies, waits for them, and re-layouts: 0.01 us -> 7.81 us  [the longest x2 4.82 us: on_device(): s_gu[..., FS:]]
    convert_element_type x5 -> x0, other arithmetic: 7.05 us -> none  [the longest x1 3.41 us: on_device(): do, = gather([dh1.astype(BF)], [], 3, 'gather_do')]
    reduce_sum x3 -> x0, other arithmetic: 6.55 us -> none  [rms_scale(): return lax.rsqrt(jnp.mean(v * v, axis=-1, keepdims=True) + EPSILON)]
    unnamed x49 -> x28, local copies, waits for them, and re-layouts: 12.7 us -> 10.6 us
where the time goes in v2:
time: 284 us
  Pallas kernels  246 us (87%)
  local copies, waits for them, and re-layouts  25.4 us (9%)
  other arithmetic  5.63 us (2%)
  matrix products  5.54 us (2%)
    pallas_call x1, Pallas kernels, conv_back(): pl.pallas_call(conv_back_kernel, out_shape=[shape((ROWS, D), F32)] + [sha...  91.9 us
    pallas_call x1, Pallas kernels, ffn(): pl.pallas_call(ffn_kernel, out_shape=[shape((ROWS, D), BF), shape((ROWS,...  81.8 us
    pallas_call x1, Pallas kernels, front(): pl.pallas_call(front_kernel, out_shape=[shape((TEAM, ROWS, D), BF), shape...  72.3 us
    unnamed x28, local copies, waits for them, and re-layouts  10.6 us

profile of v2, /device:TPU:1, one launch (start us, length us, event | category | flops | bytes accessed | tf_op | source)
XLA Modules:
  0.0 283.5 jit_solution(940729776868029882)
XLA Ops:
  0.7 1.2 copy-done
  1.9 2.8 fusion.2
  4.7 2.8 fusion.3
  7.5 0.8 pad_maximum_fusion.gu_own
  8.3 0.9 constant_dynamic-slice_fusion.2
  9.2 0.7 pad.8.down_own
  9.9 0.8 constant_dynamic-slice_fusion.5
  12.1 72.3 %front.1 = (bf16[8,256,1024]{2,1,0:T(8,128)(2,1)}, bf16[8,256,1024]{2,1,0:T(8,128)(2,1)}, bf16[1024,384]{1,0:T(8,128)(2,1)}, bf16[8,128,1024]{2,1,0:T(8,128)(2,1...) custom-call(bf16[256,1024]{1,0:T(8,128)(2,1)} %tokens.1, ...), custom_call_target="tpu_custom_call" | custom-call | tf_op jit(solution)/shard_map/front/pallas_call | solution.py:348
  84.4 1.4 fusion.13
  85.9 81.8 %ffn.1 = (bf16[256,1024]{1,0:T(8,128)(2,1)}, f32[256,1024]{1,0:T(8,128)}, bf16[8,256,1024]{2,1,0:T(8,128)(2,1)}, bf16[1024,1280]{1,0:T(8,128)(2,1)}, bf16[640,1024]{1,0:T(8,128)(2,1)}, /*index=5*/f32[1,1024]{1,0:T(1,128)}) custom-call(bf16[8,256,1024]{2,1,0:T(8,128)(2,1)} %get-tuple-element.32.tok_hbm, bf16[8,256,1024]{2,1,0:T(8,128)(2,1)} %get-tuple-element.33.e_hbm, ...), custom_call_target="tpu_custom_call" | custom-call | tf_op jit(solution)/shard_map/ffn/pallas_call | solution.py:563
  167.8 1.4 maximum_maximum_fusion.gains
  169.1 1.7 constant_dynamic-slice_fusion.1.w_out_t
  170.8 0.8 slice.35
  172.2 91.9 %conv_back.1 = (f32[256,1024]{1,0:T(8,128)}, bf16[8,128,1280]{2,1,0:T(8,128)(2,1)}, bf16[8,80,1024]{2,1,0:T(8,128)(2,1)}, bf16[8,128,384]{2,1,0:T(8,128)(2,1)}, ...) custom-call(bf16[8,256,1024]{2,1,0:T(8,128)(2,1)} %get-tuple-element.32.tok_hbm, ...), custom_call_target="tpu_custom_call" | custom-call | tf_op jit(solution)/shard_map/conv_back/pallas_call | solution.py:756
  264.1 3.1 %fusion.12 = (bf16[8,128,640]{2,1,0:T(8,128)(2,1)}, bf16[8,128,640]{2,1,0:T(8,128)(2,1)S(1)}) fusion(bf16[8,128,1280]{2,1,0:T(8,128)(2,1)} %get-tuple-element.52), kind=kLoop, calls=%fused_computation.34 | loop fusion | bytes 5242880 | tf_op jit(solution)/shard_map/slice | solution.py:846
  267.1 0.8 copy.41
  268.3 2.0 copy.47
  270.3 1.8 copy.43
  272.4 2.0 copy.48
  274.8 1.6 copy.45
  276.5 1.8 bitcast_convert_fusion
  278.6 1.0 copy.46
  280.7 1.9 copy.53
  282.5 1.0 copy.54
  (44 shorter events, 4.7 us)
Async XLA Ops:
  0.6 1.3 copy-start
  1.9 2.8 copy-start.10
  4.7 6.7 %copy-start.7 = (bf16[3,128]{1,0:T(4,128)(2,1)S(1)}, bf16[3,128]{1,0:T(4,128)(2,1)}, u32[]{:S(2)}) copy-start(bf16[3,128]{1,0:T(4,128)(2,1)} %param.13) | copy-start | bytes 2308
  4.7 6.7 %copy-start.8 = (bf16[128]{0:T(256)(128)(2,1)S(1)}, bf16[128]{0:T(256)(128)(2,1)}, u32[]{:S(2)}) copy-start(bf16[128]{0:T(256)(128)(2,1)} %param.15) | copy-start | bytes 772
  4.7 6.7 %copy-start.9 = (bf16[128]{0:T(256)(128)(2,1)S(1)}, bf16[128]{0:T(256)(128)(2,1)}, u32[]{:S(2)}) copy-start(bf16[128]{0:T(256)(128)(2,1)} %param.11) | copy-start | bytes 772
  272.4 2.0 copy-start.4
  274.8 1.6 copy-start.2
  276.4 1.9 copy-start.5
  276.5 3.0 %copy-start.6 = (f32[8,16,128]{2,1,0:T(8,128)S(1)}, f32[8,16,128]{2,1,0:T(8,128)}, u32[]{:S(2)}) copy-start(f32[8,16,128]{2,1,0:T(8,128)} %get-tuple-element.49) | copy-start | bytes 196612
  278.3 4.2 %copy-start.3 = (f32[256,1024]{1,0:T(8,128)S(1)}, f32[256,1024]{1,0:T(8,128)}, u32[]{:S(2)}) copy-start(f32[256,1024]{1,0:T(8,128)} %get-tuple-element.100) | copy-start | bytes 3145732
  278.3 5.2 %copy-start.1 = (bf16[128,4608]{1,0:T(8,128)(2,1)S(1)}, bf16[128,4608]{1,0:T(8,128)(2,1)}, u32[]{:S(2)}) copy-start(bf16[128,4608]{1,0:T(8,128)(2,1)} %param.16) | copy-start | bytes 3538948

commit v3 on v2

--- a/solution.py
+++ b/solution.py
@@ -105,16 +105,27 @@
             self.onward[i].start()
             self.handed[i].start()
 
-    def finish(self):
+    def near_done(self):
+        self.own.wait()
+        self.pair.wait()
+        for copy in self.handed[:2]:
+            copy.wait()
+
+    def hand(self):
         for i in range(2):
             self.far[i].wait_recv()
             self.handed[2 + i].start()
-        self.own.wait()
-        self.pair.wait()
+
+    def far_done(self):
         for copy in self.out + self.onward:
             copy.wait_send()
-        for copy in self.handed:
+        for copy in self.handed[2:]:
             copy.wait()
+
+    def finish(self):
+        self.hand()
+        self.near_done()
+        self.far_done()
 
 
 def block_part(ref):
@@ -190,10 +201,10 @@
             copy.wait_send()
 
 
-class GroupSum:
-    def __init__(self, share, out, half_land, land, z_land, stage, send, recv, tsend, trecv, local):
+class RingSum:
+    def __init__(self, share, half_land, land, send, recv):
         x, zh, zl, y, c = coords()
-        self.share, self.half_land, self.land, self.z_land, self.stage = share, half_land, land, z_land, stage
+        self.share, self.half_land, self.land = share, half_land, land
         right, left = device((x + 1) % 4, zh, zl, y, c), device((x + 3) % 4, zh, zl, y, c)
         far, self.near, self.back = 2 * ((x + 2) % 4), 2 * ((x + 1) % 4), 2 * ((x + 3) % 4)
         self.here, self.zh = 2 * x, zh
@@ -202,11 +213,8 @@
             (share.at[far + 1], half_land.at[1], left),
             (share.at[pl.ds(self.near, 2)], land.at[0], right),
             (share.at[pl.ds(self.back, 2)], land.at[1], left),
-            (stage.at[0], z_land.at[0], device(x, 1 - zh, zl, y, c)),
-            (stage.at[1], z_land.at[1], device(x, zh, 1 - zl, y, c)),
         ]
         self.hops = [remote(src, dst, send.at[k], recv.at[k], to) for k, (src, dst, to) in enumerate(moves)]
-        self.gather = TeamGather(stage.at[2], block_part(out), tsend, trecv, local)
 
     def far_out(self):
         self.hops[0].start()
@@ -221,40 +229,56 @@
         share[self.back + 1] = (share[self.back + 1].astype(F32) + self.half_land[1].astype(F32)).astype(kind)
         self.hops[3].start()
 
-    def ring_total(self, k):
-        return self.share[self.here + k].astype(F32) + self.land[0, k].astype(F32) + self.land[1, k].astype(F32)
-
-    def z_out(self):
+    def totals(self, both):
         self.hops[2].wait_recv()
         self.hops[3].wait_recv()
-        self.stage[0] = self.ring_total(1 - self.zh).astype(self.stage.dtype)
-        self.hops[4].start()
-
-    def z_lo_out(self):
-        own = self.ring_total(self.zh)
-        self.hops[4].wait()
-        self.stage[1] = (own + self.z_land[0].astype(F32)).astype(self.stage.dtype)
-        self.hops[5].start()
-
-    def team_out(self):
-        self.hops[5].wait()
-        self.stage[2] = (self.stage[1].astype(F32) + self.z_land[1].astype(F32)).astype(self.stage.dtype)
-        self.gather.start()
+        for i, k in enumerate((1 - self.zh, self.zh)):
+            total = self.share[self.here + k].astype(F32)
+            total += self.land[0, k].astype(F32) + self.land[1, k].astype(F32)
+            both[i] = total.astype(both.dtype)
 
     def finish(self):
-        self.gather.finish()
-        for k in range(4):
-            self.hops[k].wait_send()
+        for hop in self.hops:
+            hop.wait_send()
 
     @staticmethod
     def scratch(r, w, kind):
         return [
             pltpu.VMEM((2, r, w), kind),
             pltpu.VMEM((2, 2, r, w), kind),
+            pltpu.SemaphoreType.DMA((4,)),
+            pltpu.SemaphoreType.DMA((4,)),
+        ]
+
+
+class PartnerSum:
+    def __init__(self, both, out, land, stage, send, recv, tsend, trecv, local):
+        x, zh, zl, y, c = coords()
+        self.both, self.land, self.stage = both, land, stage
+        self.high = remote(both.at[0], land.at[0], send.at[0], recv.at[0], device(x, 1 - zh, zl, y, c))
+        self.low = remote(stage.at[0], land.at[1], send.at[1], recv.at[1], device(x, zh, 1 - zl, y, c))
+        self.gather = TeamGather(stage.at[1], block_part(out), tsend, trecv, local)
+
+    def z_out(self):
+        self.high.start()
+
+    def z_lo_out(self):
+        self.high.wait()
+        self.stage[0] = (self.both[1].astype(F32) + self.land[0].astype(F32)).astype(self.stage.dtype)
+        self.low.start()
+
+    def team_out(self):
+        self.low.wait()
+        self.stage[1] = (self.stage[0].astype(F32) + self.land[1].astype(F32)).astype(self.stage.dtype)
+        self.gather.start()
+
+    @staticmethod
+    def scratch(r, w, kind):
+        return [
             pltpu.VMEM((2, r, w), kind),
-            pltpu.VMEM((3, r, w), kind),
-            pltpu.SemaphoreType.DMA((6,)),
-            pltpu.SemaphoreType.DMA((6,)),
+            pltpu.VMEM((2, r, w), kind),
+            pltpu.SemaphoreType.DMA((2,)),
+            pltpu.SemaphoreType.DMA((2,)),
             pltpu.SemaphoreType.DMA((9,)),
             pltpu.SemaphoreType.DMA((9,)),
             pltpu.SemaphoreType.DMA(()),
@@ -269,9 +293,9 @@
 
 
 def front_kernel(
-    tokens, cotangent, small_own, in_own, out_own, gu_own, down_own,
+    tokens, cotangent, gain_one, in_weight, taps_own, out_own, gain_two, gate_weight, up_weight, down_weight,
     tok, e, w_in, w_out, w_gu, w_down, gains, p, v, z,
-    small, z_own, tsend, trecv, gsend, grecv, local, hsend, hrecv,
+    small, small_own, in_own, gu_own, down_own, z_own, tsend, trecv, gsend, grecv, local, hsend, hrecv,
 ):
     x, zh, zl, y, c = coords()
     member = 2 * y + c
@@ -284,8 +308,8 @@
         lambda k: small.at[k],
         lambda k: w_in.at[pl.ds(pl.multiple_of(k * 128, 128), 128)],
         lambda k: w_out.at[k, out_rows],
-        lambda k: w_gu.at[pl.ds(pl.multiple_of(k * 128, 128), 128)],
-        lambda k: w_down.at[pl.ds(pl.multiple_of(k * PAD, PAD), PAD)],
+        lambda k: w_gu.at[k],
+        lambda k: w_down.at[k],
     ]
     owned = [small_own, in_own, out_own.at[out_rows], gu_own, down_own]
     jobs = [
@@ -293,30 +317,55 @@
         for i, (src, slot) in enumerate(zip(owned, slots))
     ]
     tok_job.start()
-    for job in jobs:
+    rows = [gain_one[...].astype(F32), gain_two[...].astype(F32), taps_own[...].astype(F32)]
+    small_own[...] = jnp.concatenate(rows + [jnp.zeros((11, 128), F32)], axis=0).astype(BF)
+    for part in range(3):
+        in_own[:, 128 * part : 128 * part + 128] = in_weight[
+            :, pl.ds(pl.multiple_of(part * D + member * 128, 128), 128)
+        ]
+    for job in jobs[:3]:
+        job.start()
+    place = lax.broadcasted_iota(jnp.int32, (576, PAD), 1)
+    source = lax.broadcasted_iota(jnp.int32, (576, PAD), 0)
+    chosen = ((place < SEG) & (source == member * SEG + place)).astype(F32).astype(BF)
+    for half, weight in ((0, gate_weight), (FS, up_weight)):
+        for g in range(8):
+            gu_own[:, half + PAD * g : half + PAD * g + PAD] = dot(
+                weight[:, 576 * g : 576 * g + 576], chosen
+            ).astype(BF)
+    down_own[...] = contract_rows(chosen, down_weight[...]).astype(BF)
+    for job in jobs[:3]:
+        job.step()
+    for job in jobs[:3]:
+        job.relay()
+    for job in jobs[3:]:
         job.start()
     tok_job.step()
     e_job.start()
-    for job in jobs[:3]:
-        job.step()
-    jobs[0].relay()
-    jobs[1].relay()
-    tok_job.finish()
     jobs[0].finish()
     jobs[1].finish()
-    for job in jobs[3:]:
-        job.step()
-    jobs[2].relay()
     for g in range(8):
         gains[:, 128 * g : 128 * g + 128] = small[g].astype(F32)
     taps = gains[:, pl.ds(pl.multiple_of(member * 128, 128), 128)]
 
-    def project(b, last):
-        rows = pl.ds(pl.multiple_of(b * ROWS, ROWS), ROWS)
+    def project(i, carry):
+        b = 2 * ((y + pick(i // 2, (0, 1, 3, 2))) % 4) + i % 2
         h0 = tok[b].astype(F32)
         n1 = (h0 * rms_scale(h0) * gains[0:1]).astype(BF)
-        block = dot(n1, w_in[...])
-        p[rows] = block
+        p[pl.ds(pl.multiple_of(b * ROWS, ROWS), ROWS)] = dot(n1, w_in[...])
+        return carry
+
+    tok_job.near_done()
+    lax.fori_loop(0, 6, project, 0)
+    tok_job.hand()
+    tok_job.far_done()
+    lax.fori_loop(6, 8, project, 0)
+    for job in jobs[3:]:
+        job.step()
+
+    def convolve(b, last):
+        rows = pl.ds(pl.multiple_of(b * ROWS, ROWS), ROWS)
+        block = p[rows]
         mixed = block[:, :128] * block[:, 256:]
         behind = jnp.concatenate([last, mixed], axis=0)
         conv = taps[2:3] * behind[6 : ROWS + 6] + taps[3:4] * behind[7 : ROWS + 7] + taps[4:5] * behind[8:]
@@ -324,7 +373,7 @@
         z_own[rows] = (block[:, 128:256] * conv).astype(BF)
         return mixed[ROWS - 8 :]
 
-    lax.fori_loop(0, 8, project, jnp.zeros((8, 128), F32))
+    lax.fori_loop(0, 8, convolve, jnp.zeros((8, 128), F32))
     z_job.start()
     e_job.step()
     jobs[3].relay()
@@ -342,7 +391,7 @@
     remote(w_out.at[:, out_rows], w_out.at[:, other_rows], hsend, hrecv, device(x, zh, zl, y, 1 - c)).wait_recv()
 
 
-def front(tokens, cotangent, small_own, in_own, out_own, gu_own, down_own, collective_id, name):
+def front(args, collective_id, name):
     vmem, anywhere = pl.BlockSpec(memory_space=pltpu.VMEM), pl.BlockSpec(memory_space=pl.ANY)
     shape = jax.ShapeDtypeStruct
     return pl.pallas_call(
@@ -352,17 +401,21 @@
             shape((TEAM, ROWS, D), BF),
             shape((D, 384), BF),
             shape((8, 128, D), BF),
-            shape((D, 2 * FS), BF),
-            shape((FS, D), BF),
+            shape((8, 128, 2 * FS), BF),
+            shape((8, PAD, D), BF),
             shape((16, D), F32),
             shape((T, 384), F32),
             shape((T, 128), F32),
             shape((T, D), BF),
         ],
-        in_specs=[anywhere] * 7,
+        in_specs=[vmem] * 10,
         out_specs=[vmem, anywhere, vmem, anywhere, anywhere, anywhere, vmem, vmem, vmem, anywhere],
         scratch_shapes=[
             pltpu.VMEM((8, 16, 128), BF),
+            pltpu.VMEM((16, 128), BF),
+            pltpu.VMEM((128, 384), BF),
+            pltpu.VMEM((128, 2 * FS), BF),
+            pltpu.VMEM((PAD, D), BF),
             pltpu.VMEM((T, 128), BF),
             pltpu.SemaphoreType.DMA((3, 9)),
             pltpu.SemaphoreType.DMA((3, 9)),
@@ -376,7 +429,7 @@
             collective_id=collective_id, has_side_effects=True, vmem_limit_bytes=VLIM
         ),
         name=name,
-    )(tokens, cotangent, small_own, in_own, out_own, gu_own, down_own)
+    )(*args)
 
 
 class TeamSum:
@@ -448,9 +501,9 @@
 
 def ffn_kernel(
     tok_hbm, e_hbm, z_hbm, w_out_hbm, w_gu_hbm, w_down_hbm, gain_ref,
-    block_out, dh1_out, do_hbm, d_gu, d_down, gain_grad,
+    block_out, dh1_out, do_hbm, gu_both, down_both, gain_grad,
     tok, e, z, w_out, w_gu, w_down, n2, a, dgq, h1_ref, do_own, share, local, wlocal, blocal,
-    dsend, drecv, pair_land, half_land, land, psend, precv, send, recv,
+    dsend, drecv, pair_land, half_land, land, psend, precv, send, recv, *rings,
 ):
     x, zh, zl, y, c = coords()
     weights = [
@@ -463,8 +516,8 @@
         pair, rows = pl.ds(2 * k, 2), pl.ds(pl.multiple_of(2 * ROWS * k, 2 * ROWS), 2 * ROWS)
         blocks.append(
             [
-                pltpu.make_async_copy(z_hbm.at[rows], z.at[rows], blocal.at[s, 0]),
-                pltpu.make_async_copy(tok_hbm.at[pair], tok.at[pair], blocal.at[s, 1]),
+                pltpu.make_async_copy(z_hbm.at[rows], z.at[s % 2], blocal.at[s, 0]),
+                pltpu.make_async_copy(tok_hbm.at[pair], tok.at[s % 2], blocal.at[s, 1]),
                 pltpu.make_async_copy(e_hbm.at[pair], e.at[pair], blocal.at[s, 2]),
             ]
         )
@@ -473,10 +526,12 @@
         copy.start()
     for copy in weights[1:]:
         copy.start()
-    for copies in blocks[1:]:
-        for copy in copies:
-            copy.start()
-    meet(team_peers())
+    for s, copies in enumerate(blocks[1:]):
+        for i, copy in enumerate(copies):
+            if i == 2 or s == 0:
+                copy.start()
+    meet(team_peers() + x_peers())
+    gu, down = RingSum(w_gu, *rings[:4]), RingSum(w_down, *rings[4:])
     sums = [
         TeamSum(
             share.at[k], pair_land.at[k], half_land.at[k], land.at[k],
@@ -486,75 +541,96 @@
     ]
     for copy in weights:
         copy.wait()
-    gain = gain_ref[...]
+    gain = gain_ref[1:2]
     gain_grad[...] = jnp.zeros_like(gain_grad)
 
-    def step(i, carry):
+    def step(s, carry):
         for k in range(4):
 
-            @pl.when(i == 2 * k)
+            @pl.when(s == k)
             def _():
                 for copy in blocks[k]:
                     copy.wait()
-
-        s, own = i // 2, i % 2
-        turn = jnp.where(s == 0, 2, jnp.where(s == 1, 1, jnp.where(s == 2, 3, 0)))
-        b = 2 * ((y + turn) % 4) + jnp.where(own == 1, c, 1 - c)
-        rows = pl.ds(pl.multiple_of(b * ROWS, ROWS), ROWS)
-        h1 = tok[b].astype(F32) + dot(z[rows, :], w_out[...])
-        h1_ref[...] = h1
-        hs = h1 * lax.rsqrt(jnp.mean(h1 * h1, axis=-1, keepdims=True) + EPSILON)
-        n2_b = (hs * gain).astype(BF)
+                if k in (1, 2):
+                    for copy in blocks[k + 1][:2]:
+                        copy.start()
+
+        chip = (y + pick(s, (2, 1, 3, 0))) % 4
+        rows = pl.ds(pl.multiple_of(2 * ROWS * chip, 2 * ROWS), 2 * ROWS)
+        h1 = tok[s % 2].reshape(2 * ROWS, D).astype(F32) + dot(z[s % 2], w_out[...])
+        h1_ref[...] = h1.reshape(2, ROWS, D)
+        n2_b = (h1 * rms_scale(h1) * gain).astype(BF)
         n2[rows, :] = n2_b
-        g = dot(n2_b, w_gu[:, :FS])
-        q = dot(n2_b, w_gu[:, FS:])
+        g = dot(n2_b, w_gu[:, :, :FS].reshape(D, FS))
+        q = dot(n2_b, w_gu[:, :, FS:].reshape(D, FS))
         sig = jax.nn.sigmoid(g)
         act = g * sig
-        a_b = (act * q).astype(BF)
-        a[rows, :] = a_b
-        da = back_project(e[b], w_down[...])
+        a[rows, :] = (act * q).astype(BF)
+        da = back_project(e[pl.ds(2 * chip, 2)].reshape(2 * ROWS, D), w_down[...].reshape(FS, D))
         dgq[rows, :FS] = (da * q * sig * (1.0 + g * (1.0 - sig))).astype(BF)
         dgq[rows, FS:] = (da * act).astype(BF)
-        share[1, b] = dot(a_b, w_down[...]).astype(BF)
-        dn2 = back_project(dgq[rows, :], w_gu[...])
-        share[0, b] = dn2.astype(BF)
-        scale = lax.rsqrt(jnp.mean(h1_ref[...] * h1_ref[...], axis=-1, keepdims=True) + EPSILON)
-        gain_grad[...] += jnp.sum(dn2 * (h1_ref[...] * scale), axis=0, keepdims=True)
-        for k in range(4):
-
-            @pl.when(i == 2 * k)
+        for k in range(1, 4):
+
+            @pl.when(s == k)
             def _():
-                sums[0].send_pair(k)
-                sums[1].send_pair(k)
-
-            @pl.when(i == 2 * k + 1)
-            def _():
-                sums[0].add_pair(k)
-                sums[1].add_pair(k)
+                sums[0].add_pair(k - 1)
+
+        for own in range(2):
+            core = c if own else 1 - c
+            b = 2 * chip + core
+            block = pl.ds(pl.multiple_of(b * ROWS, ROWS), ROWS)
+            dn2 = back_project(dgq[block, :], w_gu[...].reshape(D, 2 * FS))
+            share[0, b] = dn2.astype(BF)
+            h1 = h1_ref[core]
+            gain_grad[...] += jnp.sum(dn2 * (h1 * rms_scale(h1)), axis=0, keepdims=True)
+            share[1, b] = dot(a[block, :], w_down[...].reshape(FS, D)).astype(BF)
+            for k in range(4):
+
+                @pl.when(s == k)
+                def _():
+                    if own:
+                        if k:
+                            sums[1].add_pair(k - 1)
+                    else:
+                        sums[0].send_pair(k)
+                        sums[1].send_pair(k)
 
         return carry
 
-    lax.fori_loop(0, 8, step, 0)
-
-    d_down[...] = contract_rows(a[...], e[...].reshape(T, D)).astype(BF)
+    lax.fori_loop(0, 4, step, 0)
+
+    def tile(i, carry):
+        m = (((x + 2) % 4) // 2 + i) % 2
+        columns = pl.ds(pl.multiple_of(m * 512, 512), 512)
+        w_gu[pl.ds(4 * m, 4)] = contract_rows(n2[:, columns], dgq[...]).astype(BF).reshape(4, 128, 2 * FS)
+
+        @pl.when(i == 0)
+        def _():
+            gu.far_out()
+
+        return carry
+
+    lax.fori_loop(0, 2, tile, 0)
+    sums[0].add_pair(3)
+    w_down[...] = contract_rows(a[...], e[...].reshape(T, D)).astype(BF).reshape(8, PAD, D)
+    gu.near_out()
+    down.far_out()
     dn2 = sums[0].result()
-    h1 = h1_ref[...]
-    s2 = lax.rsqrt(jnp.mean(h1 * h1, axis=-1, keepdims=True) + EPSILON)
-    dh1 = e[2 * y + c].astype(F32) + norm_reverse(h1, s2, gain, dn2)
+    h1 = h1_ref[c]
+    dh1 = e[2 * y + c].astype(F32) + norm_reverse(h1, rms_scale(h1), gain, dn2)
     dh1_out[...] = dh1
     do_own[...] = dh1.astype(BF)
     do_job = TeamGather(do_own, block_part(do_hbm), dsend, drecv, local)
     do_job.start()
-
-    def tile(m, carry):
-        columns = pl.ds(pl.multiple_of(m * 512, 512), 512)
-        d_gu[columns, :] = contract_rows(n2[:, columns], dgq[...]).astype(BF)
-        return carry
-
-    lax.fori_loop(0, 2, tile, 0)
+    sums[1].add_pair(3)
+    down.near_out()
     do_job.step()
-    block_out[...] = (h1_ref[...] + sums[1].result()).astype(BF)
+    block_out[...] = (h1_ref[c] + sums[1].result()).astype(BF)
     do_job.finish()
+    gu.totals(gu_both)
+    down.totals(down_both)
+    gu.finish()
+    down.finish()
 
 
 def ffn(tok, e, z, w_out, w_gu, w_down, gain, collective_id, name):
@@ -566,23 +642,23 @@
             shape((ROWS, D), BF),
             shape((ROWS, D), F32),
             shape((TEAM, ROWS, D), BF),
-            shape((D, 2 * FS), BF),
-            shape((FS, D), BF),
+            shape((2, 128, 2 * FS), BF),
+            shape((2, PAD, D), BF),
             shape((1, D), F32),
         ],
         in_specs=[anywhere] * 6 + [vmem],
         out_specs=[vmem, vmem, anywhere, vmem, vmem, vmem],
         scratch_shapes=[
+            pltpu.VMEM((2, 2, ROWS, D), BF),
             pltpu.VMEM((TEAM, ROWS, D), BF),
-            pltpu.VMEM((TEAM, ROWS, D), BF),
-            pltpu.VMEM((T, D), BF),
+            pltpu.VMEM((2, 2 * ROWS, D), BF),
             pltpu.VMEM((D, D), BF),
-            pltpu.VMEM((D, 2 * FS), BF),
-            pltpu.VMEM((FS, D), BF),
+            pltpu.VMEM((8, 128, 2 * FS), BF),
+            pltpu.VMEM((8, PAD, D), BF),
             pltpu.VMEM((T, D), BF),
             pltpu.VMEM((T, FS), BF),
             pltpu.VMEM((T, 2 * FS), BF),
-            pltpu.VMEM((ROWS, D), F32),
+            pltpu.VMEM((2, ROWS, D), F32),
             pltpu.VMEM((ROWS, D), BF),
             pltpu.VMEM((2, TEAM, ROWS, D), BF),
             pltpu.SemaphoreType.DMA(()),
@@ -591,7 +667,9 @@
             pltpu.SemaphoreType.DMA((9,)),
             pltpu.SemaphoreType.DMA((9,)),
         ]
-        + TeamSum.scratch(2),
+        + TeamSum.scratch(2)
+        + RingSum.scratch(128, 2 * FS, BF)
+        + RingSum.scratch(PAD, D, BF),
         compiler_params=pltpu.CompilerParams(
             collective_id=collective_id, has_side_effects=True, vmem_limit_bytes=VLIM
         ),
@@ -600,33 +678,40 @@
 
 
 def conv_back_kernel(
-    tok_hbm, do_hbm, z_hbm, d_gu_hbm, d_down_hbm, w_in, w_out_t, p, v, dh1, gains, taps,
+    tok_hbm, do_hbm, z_hbm, w_out_hbm, gu_both, down_both, w_in, p, v, dh1, gains, gain_two_grad,
     token_grad, gu_out, down_out, in_out, out_out, small_out,
-    tok, do, z, d_gu, d_down, d_in, d_out, d_small, n1, up, dv, dp, sums, share, local, *rest,
+    tok, do, z, d_in, d_out, d_small, in_both, out_both, small_both, w_out_t, n1, up, dv, dp, sums, share, local, *rest,
 ):
     x, zh, zl, y, c = coords()
     member = 2 * y + c
-    here = x * 2 + zh
     meet(team_peers() + x_peers() + [device(x, 1 - zh, zl, y, c), device(x, zh, 1 - zl, y, c)])
     loads = [
         pltpu.make_async_copy(src, dst, local.at[i])
         for i, (src, dst) in enumerate(
-            ((d_gu_hbm, d_gu), (d_down_hbm, d_down), (do_hbm, do), (z_hbm, z), (tok_hbm, tok))
+            (
+                (w_out_hbm.at[pl.ds(pl.multiple_of(member * 128, 128), 128)], w_out_t),
+                (do_hbm, do),
+                (tok_hbm, tok),
+                (z_hbm, z),
+            )
         )
     ]
     for copy in loads:
         copy.start()
     dn1_sum = TeamSum(share, *[ref.at[0] for ref in rest[:7]])
-    parts = ((d_gu, gu_out), (d_down, down_out), (d_in, in_out), (d_out, out_out), (d_small, small_out))
-    jobs = [
-        GroupSum(ref, out, *rest[7 + 9 * i : 16 + 9 * i]) for i, (ref, out) in enumerate(parts)
+    in_ring, out_ring, small_ring = [
+        RingSum(ref, *rest[7 + 4 * i : 11 + 4 * i]) for i, ref in enumerate((d_in, d_out, d_small))
     ]
+    parts = (
+        (gu_both, gu_out), (down_both, down_out), (in_both, in_out), (out_both, out_out), (small_both, small_out)
+    )
+    jobs = [PartnerSum(*part, *rest[19 + 7 * i : 26 + 7 * i]) for i, part in enumerate(parts)]
     gu, down, in_job, out_job, small = jobs
+    gu.z_out()
+    down.z_out()
     loads[0].wait()
-    gu.far_out()
     loads[1].wait()
-    down.far_out()
-    loads[2].wait()
+    taps = gains[:, pl.ds(pl.multiple_of(member * 128, 128), 128)]
 
     up[pl.ds(0, 8)] = jnp.zeros((8, 128), F32)
     dv[pl.ds(T, 8)] = jnp.zeros((8, 128), F32)
@@ -640,33 +725,27 @@
         return carry
 
     lax.fori_loop(0, 8, first, 0)
+    loads[2].wait()
     sums[...] = jnp.zeros_like(sums)
 
     def second(b, carry):
         rows = pl.ds(pl.multiple_of(b * ROWS, ROWS), ROWS)
         longer = pl.ds(pl.multiple_of(b * ROWS, ROWS), ROWS + 8)
         ahead, behind = dv[longer], up[longer]
-        du = taps[0:1] * ahead[2 : ROWS + 2] + taps[1:2] * ahead[1 : ROWS + 1] + taps[2:3] * ahead[:ROWS]
+        du = taps[2:3] * ahead[2 : ROWS + 2] + taps[3:4] * ahead[1 : ROWS + 1] + taps[4:5] * ahead[:ROWS]
         dp[rows, :128] = (du * p[rows, 256:]).astype(BF)
         dp[rows, 256:] = (du * p[rows, :128]).astype(BF)
         for k in range(3):
             sums[2 + k : 3 + k, :128] += jnp.sum(
                 ahead[:ROWS] * behind[6 + k : 6 + k + ROWS], axis=0, keepdims=True
             )
+        h0 = tok[b].astype(F32)
+        n1[rows, :] = (h0 * rms_scale(h0) * gains[0:1]).astype(BF)
         return carry
 
     lax.fori_loop(0, 8, second, 0)
-    gu.near_out()
-    down.near_out()
-    loads[3].wait()
-    d_out[...] = (
-        contract_rows(z[...], do[:, :, pl.ds(pl.multiple_of(member * 128, 128), 128)].reshape(T, 128))
-        .astype(BF)
-        .reshape(8, 128, 128)
-    )
-    out_job.far_out()
-    loads[4].wait()
-
+    gu.z_lo_out()
+    down.z_lo_out()
     def third(i, carry):
         s, own = i // 2, i % 2
         turn = jnp.where(s == 0, 2, jnp.where(s == 1, 1, jnp.where(s == 2, 3, 0)))
@@ -674,7 +753,6 @@
         rows = pl.ds(pl.multiple_of(b * ROWS, ROWS), ROWS)
         h0 = tok[b].astype(F32)
         hs = h0 * rms_scale(h0)
-        n1[rows, :] = (hs * gains[0:1]).astype(BF)
         dn1 = back_project(dp[rows, :], w_in[...])
         share[b] = dn1.astype(BF)
         sums[0:1] += jnp.sum(dn1 * hs, axis=0, keepdims=True)
@@ -691,39 +769,55 @@
         return carry
 
     lax.fori_loop(0, 8, third, 0)
+    gu.team_out()
     d_in[...] = contract_rows(n1[...], dp[...]).astype(BF).reshape(8, 128, 384)
-    in_job.far_out()
+    in_ring.far_out()
+    down.team_out()
+    loads[3].wait()
+    d_out[...] = (
+        contract_rows(z[...], do[:, :, pl.ds(pl.multiple_of(member * 128, 128), 128)].reshape(T, 128))
+        .astype(BF)
+        .reshape(8, 128, 128)
+    )
+    out_ring.far_out()
     conv = sums[2:5, :128]
     for g in range(8):
         d_small[g] = jnp.zeros((16, 128), F32)
         d_small[g, 0:1] = sums[0:1, 128 * g : 128 * g + 128]
-        d_small[g, 1:2] = gains[1:2, 128 * g : 128 * g + 128]
+        d_small[g, 1:2] = gain_two_grad[:, 128 * g : 128 * g + 128]
         d_small[g, 2:5] = jnp.where(member == g, conv, 0.0)
-    small.far_out()
-    out_job.near_out()
-    gu.z_out()
-    down.z_out()
-    in_job.near_out()
-    small.near_out()
+    small_ring.far_out()
+    in_ring.near_out()
+    gu.gather.step()
+    out_ring.near_out()
+    small_ring.near_out()
+    down.gather.step()
+    in_ring.totals(in_both)
+    in_job.z_out()
+    out_ring.totals(out_both)
     out_job.z_out()
-    gu.z_lo_out()
-    down.z_lo_out()
+    small_ring.totals(small_both)
+    small.z_out()
+    gu.gather.hand()
+    in_job.z_lo_out()
+    out_job.z_lo_out()
+    down.gather.hand()
+    in_job.team_out()
+    small.z_lo_out()
+    out_job.team_out()
+    small.team_out()
+    late = (in_job, out_job, small)
+    for job in late:
+        job.gather.step()
     h0 = tok[member].astype(F32)
     token_grad[...] = dh1[...] + norm_reverse(h0, rms_scale(h0), gains[0:1], dn1_sum.result())
-    gu.team_out()
-    down.team_out()
-    out_job.z_lo_out()
-    in_job.z_out()
-    small.z_out()
-    in_job.z_lo_out()
-    small.z_lo_out()
-    out_job.team_out()
-    in_job.team_out()
-    small.team_out()
+    for job in late:
+        job.gather.hand()
     for job in jobs:
-        job.gather.step()
-    for job in jobs:
-        job.finish()
+        job.gather.near_done()
+        job.gather.far_done()
+    for ring in (out_ring, in_ring, small_ring):
+        ring.finish()
 
 
 def x_peers():
@@ -731,7 +825,7 @@
     return [device((x + 1) % 4, zh, zl, y, c), device((x + 3) % 4, zh, zl, y, c)]
 
 
-def conv_back(tok, do, z, d_gu, d_down, w_in, w_out_t, p, v, dh1, gains, taps, collective_id, name):
+def conv_back(args, collective_id, name):
     vmem, anywhere = pl.BlockSpec(memory_space=pltpu.VMEM), pl.BlockSpec(memory_space=pl.ANY)
     shape = jax.ShapeDtypeStruct
     blocks = [((128, 2 * FS), BF), ((PAD, D), BF), ((128, 384), BF), ((128, 128), BF), ((16, 128), F32)]
@@ -740,30 +834,86 @@
         pltpu.VMEM((TEAM, ROWS, D), BF),
         pltpu.VMEM((T, D), BF),
     ]
-    scratch += [pltpu.VMEM((8,) + block, kind) for block, kind in blocks]
+    scratch += [pltpu.VMEM((8,) + block, kind) for block, kind in blocks[2:]]
+    scratch += [pltpu.VMEM((2,) + block, kind) for block, kind in blocks[2:]]
     scratch += [
+        pltpu.VMEM((128, D), BF),
         pltpu.VMEM((T, D), BF),
         pltpu.VMEM((T + 8, 128), F32),
         pltpu.VMEM((T + 8, 128), F32),
         pltpu.VMEM((T, 384), BF),
         pltpu.VMEM((8, D), F32),
         pltpu.VMEM((TEAM, ROWS, D), BF),
-        pltpu.SemaphoreType.DMA((5,)),
+        pltpu.SemaphoreType.DMA((4,)),
     ]
     scratch += TeamSum.scratch(1)
+    for block, kind in blocks[2:]:
+        scratch += RingSum.scratch(*block, kind)
     for block, kind in blocks:
-        scratch += GroupSum.scratch(*block, kind)
+        scratch += PartnerSum.scratch(*block, kind)
     return pl.pallas_call(
         conv_back_kernel,
         out_shape=[shape((ROWS, D), F32)] + [shape((8,) + block, kind) for block, kind in blocks],
-        in_specs=[anywhere] * 5 + [vmem] * 7,
+        in_specs=[anywhere] * 4 + [vmem] * 8,
         out_specs=[vmem] + [anywhere] * 5,
         scratch_shapes=scratch,
         compiler_params=pltpu.CompilerParams(
             collective_id=collective_id, has_side_effects=True, vmem_limit_bytes=VLIM
         ),
         name=name,
-    )(tok, do, z, d_gu, d_down, w_in, w_out_t, p, v, dh1, gains, taps)
+    )(*args)
+
+
+def assemble_kernel(gu, down, w_in, w_out, small, block, token, g_in, g_out, g_gate, g_up, g_down, g_one, g_two, g_conv, b_out, t_out):
+    for t in range(TEAM):
+        for part in range(3):
+            at = part * D + 128 * t
+            g_in[:, at : at + 128] = w_in[t, :, 128 * part : 128 * part + 128].astype(F32)
+        g_out[:, 128 * t : 128 * t + 128] = w_out[t].astype(F32)
+        g_down[SEG * t : SEG * t + SEG, :] = down[t, :SEG].astype(F32)
+    total = small[0]
+    for t in range(1, TEAM):
+        total += small[t]
+    g_one[...] = total[0:1]
+    g_two[...] = total[1:2]
+    g_conv[...] = total[2:5]
+    b_out[...] = block[...]
+    t_out[...] = token[...]
+
+    def chunk(i, carry):
+        rows = pl.ds(pl.multiple_of(i * 32, 32), 32)
+        pieces = [gu[t, rows].astype(F32) for t in range(TEAM)]
+        for half, ref in ((0, g_gate), (FS, g_up)):
+            for g in range(8):
+                for t in range(TEAM):
+                    at = 576 * g + SEG * t
+                    ref[rows, at : at + SEG] = pieces[t][:, half + PAD * g : half + PAD * g + SEG]
+        return carry
+
+    lax.fori_loop(0, 4, chunk, 0)
+
+
+def assemble(gu, down, w_in, w_out, small, block, token):
+    vmem, shape = pl.BlockSpec(memory_space=pltpu.VMEM), jax.ShapeDtypeStruct
+    return pl.pallas_call(
+        assemble_kernel,
+        out_shape=[
+            shape((128, 3 * D), F32),
+            shape((128, D), F32),
+            shape((128, 8 * 576), F32),
+            shape((128, 8 * 576), F32),
+            shape((576, D), F32),
+            shape((1, 128), F32),
+            shape((1, 128), F32),
+            shape((3, 128), F32),
+            shape((ROWS, D), BF),
+            shape((ROWS, D), F32),
+        ],
+        in_specs=[vmem] * 7,
+        out_specs=[vmem] * 10,
+        compiler_params=pltpu.CompilerParams(vmem_limit_bytes=VLIM),
+        name="assemble",
+    )(gu, down, w_in, w_out, small, block, token)
 
 
 def rms_scale(v):
@@ -790,61 +940,24 @@
 def on_device(
     tokens, norm_gain, in_weight, conv_weight, out_weight, ffn_gain, gate_weight, up_weight, down_weight, cotangent
 ):
-    member = lax.axis_index("replica") % 8
-    lanes = member * 128
-
-    w_in_own = jnp.concatenate(
-        [lax.dynamic_slice_in_dim(in_weight, part * D + lanes, 128, axis=1) for part in range(3)], axis=1
-    )
-    column = lax.broadcasted_iota(jnp.int32, (8 * 576, FS), 0)
-    place = lax.broadcasted_iota(jnp.int32, (8 * 576, FS), 1)
-    chosen = (place % PAD < SEG) & (column == (place // PAD) * 576 + member * SEG + place % PAD)
-    pick = chosen.astype(BF)
-    gu_own = jnp.concatenate([dot(gate_weight, pick), dot(up_weight, pick)], axis=1).astype(BF)
-    down_own = jnp.pad(lax.dynamic_slice_in_dim(down_weight, member * SEG, SEG, axis=0), ((0, PAD - SEG), (0, 0)))
-    small_own = jnp.concatenate([norm_gain[None], ffn_gain[None], conv_weight, jnp.zeros((11, 128), BF)], axis=0)
-
     tok, e, w_in, w_out, w_gu, w_down, gains, p, v, z = front(
-        tokens, cotangent, small_own, w_in_own, out_weight, gu_own, down_own, 0, "front"
+        (
+            tokens, cotangent, norm_gain[None], in_weight, conv_weight, out_weight, ffn_gain[None],
+            gate_weight, up_weight, down_weight,
+        ),
+        0,
+        "front",
     )
     w_out = w_out.reshape(D, D)
-    block_out, dh1, do, d_gu, d_down, d_gain_two = ffn(tok, e, z, w_out, w_gu, w_down, gains[1:2], 1, "ffn")
+    block_out, dh1, do, gu_both, down_both, d_gain_two = ffn(tok, e, z, w_out, w_gu, w_down, gains, 1, "ffn")
     token_grad, s_gu, s_down, s_in, s_out, s_small = conv_back(
-        tok,
-        do,
-        z,
-        d_gu.reshape(8, 128, 2 * FS),
-        d_down.reshape(8, PAD, D),
-        w_in,
-        lax.dynamic_slice_in_dim(w_out, lanes, 128, axis=0),
-        p,
-        v,
-        dh1,
-        jnp.concatenate([gains[0:1], d_gain_two, jnp.zeros((6, D), F32)], axis=0),
-        jnp.pad(lax.dynamic_slice_in_dim(gains[2:5], lanes, 128, axis=1), ((0, 5), (0, 0))),
-        2,
-        "conv_back",
+        (tok, do, z, w_out, gu_both, down_both, w_in, p, v, dh1, gains, d_gain_two), 2, "conv_back"
     )
-
-    def columns(s):
-        s = s.reshape(8, 128, 8, PAD)[..., :SEG]
-        return s.transpose(1, 2, 0, 3).reshape(128, 8 * 576).astype(F32)
-
-    g_in = s_in.reshape(8, 128, 3, 128).transpose(1, 2, 0, 3).reshape(128, 3 * D).astype(F32)
-    g_out = s_out.transpose(1, 0, 2).reshape(128, D).astype(F32)
-    g_down = s_down[:, :SEG].reshape(576, D).astype(F32)
-    g_small = jnp.sum(s_small, axis=0)
+    g_in, g_out, g_gate, g_up, g_down, g_one, g_two, g_conv, block_out, token_grad = assemble(
+        s_gu, s_down, s_in, s_out, s_small, block_out, token_grad
+    )
     return (
-        block_out,
-        token_grad,
-        g_small[0],
-        g_in,
-        g_small[2:5],
-        g_out,
-        g_small[1],
-        columns(s_gu[..., :FS]),
-        columns(s_gu[..., FS:]),
-        g_down,
+        block_out, token_grad, g_one[0], g_in, g_conv, g_out, g_two[0], g_gate, g_up, g_down
     )
 
 

time: 284 us -> 245 us (0.86)
  local copies, waits for them, and re-layouts: 25.4 us -> 0 us
  other arithmetic: 5.63 us -> 0 us
  matrix products: 5.54 us -> 0 us
    pallas_call x1, Pallas kernels: 91.9 us -> 79.5 us  [conv_back(): pl.pallas_call(conv_back_kernel, out_shape=[shape((ROWS, D), F32)] + [sha...]
    unnamed x28 -> x0, local copies, waits for them, and re-layouts: 10.6 us -> none
    pallas_call x0 -> x1, Pallas kernels: none -> 9.3 us  [assemble(): pl.pallas_call(assemble_kernel, out_shape=[shape((128, 3 * D), F32), shap...]
    slice x7 -> x0, local copies, waits for them, and re-layouts: 8.5 us -> none  [the longest x2 4.82 us: on_device(): s_gu[..., FS:]]
    dot_general x2 -> x0, matrix products: 5.54 us -> none  [dot(): return jnp.dot(a, b, preferred_element_type=F32)]
    concatenate x4 -> x0, other arithmetic: 3.44 us -> none  [the longest x1 1.36 us: on_device(): jnp.concatenate([gains[0:1], d_gain_two, jnp.zeros((6, D), F32)], axis=0)]
    dynamic_slice x4 -> x0, local copies, waits for them, and re-layouts: 3.39 us -> none  [the longest x1 1.67 us: on_device(): lax.dynamic_slice_in_dim(w_out, lanes, 128, axis=0)]
where the time goes in v3:
time: 245 us
  Pallas kernels  244 us (100%)
    pallas_call x1, Pallas kernels, ffn(): pl.pallas_call(ffn_kernel, out_shape=[shape((ROWS, D), BF), shape((ROWS,...  80.7 us
    pallas_call x1, Pallas kernels, conv_back(): pl.pallas_call(conv_back_kernel, out_shape=[shape((ROWS, D), F32)] + [sha...  79.5 us
    pallas_call x1, Pallas kernels, front(): pl.pallas_call(front_kernel, out_shape=[shape((TEAM, ROWS, D), BF), shape...  74.9 us
    pallas_call x1, Pallas kernels, assemble(): pl.pallas_call(assemble_kernel, out_shape=[shape((128, 3 * D), F32), shap...  9.3 us

profile of v3, /device:TPU:1, one launch (start us, length us, event | category | flops | bytes accessed | tf_op | source)
XLA Modules:
  0.0 245.1 jit_solution(10152812657090546656)
XLA Ops:
  0.6 74.9 %front.1 = (bf16[8,256,1024]{2,1,0:T(8,128)(2,1)}, bf16[8,256,1024]{2,1,0:T(8,128)(2,1)}, bf16[1024,384]{1,0:T(8,128)(2,1)}, bf16[8,128,1024]{2,1,0:T(8,128)(2,1...) custom-call(bf16[256,1024]{1,0:T(8,128)(2,1)} %tokens.1, ...), custom_call_target="tpu_custom_call" | custom-call | tf_op jit(solution)/shard_map/front/pallas_call | solution.py:397
  75.6 80.7 %ffn.1 = (bf16[256,1024]{1,0:T(8,128)(2,1)}, f32[256,1024]{1,0:T(8,128)}, bf16[8,256,1024]{2,1,0:T(8,128)(2,1)}, bf16[2,128,1280]{2,1,0:T(8,128)(2,1)}, bf16[2,80,1024]{2,1,0:T(8,128)(2,1)}, /*index=5*/f32[1,1024]{1,0:T(1,128)}) custom-call(bf16[8,256,1024]{2,1,0:T(8,128)(2,1)} %get-tuple-element.42.tok_hbm, bf16[8,256,1024]{2,1,0:T(8,128)(2,1)} %get-tuple-element.43.e_hbm, ...), custom_call_target="tpu_custom_call" | custom-call | tf_op jit(solution)/shard_map/ffn/pallas_call | solution.py:639
  156.3 79.5 %conv_back.1 = (f32[256,1024]{1,0:T(8,128)}, bf16[8,128,1280]{2,1,0:T(8,128)(2,1)}, bf16[8,80,1024]{2,1,0:T(8,128)(2,1)}, bf16[8,128,384]{2,1,0:T(8,128)(2,1)}, ...) custom-call(bf16[8,256,1024]{2,1,0:T(8,128)(2,1)} %get-tuple-element.42.tok_hbm, ...), custom_call_target="tpu_custom_call" | custom-call | tf_op jit(solution)/shard_map/conv_back/pallas_call | solution.py:854
  235.8 9.3 %assemble.1 = (f32[128,3072]{1,0:T(8,128)}, f32[128,1024]{1,0:T(8,128)}, f32[128,4608]{1,0:T(8,128)}, f32[128,4608]{1,0:T(8,128)}, f32[576,1024]{1,0:T(8,128)}, ...) custom-call(bf16[8,128,1280]{2,1,0:T(8,128)(2,1)} %get-tuple-element, ...), custom_call_target="tpu_custom_call" | custom-call | tf_op jit(solution)/shard_map/assemble/pallas_call | solution.py:898

commit v4 on v3

--- a/solution.py
+++ b/solution.py
@@ -294,8 +294,9 @@
 
 def front_kernel(
     tokens, cotangent, gain_one, in_weight, taps_own, out_own, gain_two, gate_weight, up_weight, down_weight,
-    tok, e, w_in, w_out, w_gu, w_down, gains, p, v, z,
-    small, small_own, in_own, gu_own, down_own, z_own, tsend, trecv, gsend, grecv, local, hsend, hrecv,
+    tok_hbm, e, w_in_hbm, w_out, w_gu, w_down, gains, p_hbm, v_hbm, z,
+    small, small_own, in_own, gu_own, down_own, z_own, tok, w_in, p, v,
+    tsend, trecv, gsend, grecv, local, hsend, hrecv, saving,
 ):
     x, zh, zl, y, c = coords()
     member = 2 * y + c
@@ -375,6 +376,12 @@
 
     lax.fori_loop(0, 8, convolve, jnp.zeros((8, 128), F32))
     z_job.start()
+    saved = [
+        pltpu.make_async_copy(src, dst, saving.at[i])
+        for i, (src, dst) in enumerate(((tok, tok_hbm), (w_in, w_in_hbm), (p, p_hbm), (v, v_hbm)))
+    ]
+    for copy in saved:
+        copy.start()
     e_job.step()
     jobs[3].relay()
     jobs[4].relay()
@@ -387,6 +394,8 @@
     other_rows = pl.ds(pl.multiple_of(64 - c * 64, 64), 64)
     jobs[3].finish()
     jobs[4].finish()
+    for copy in saved:
+        copy.wait()
     handed.wait_send()
     remote(w_out.at[:, out_rows], w_out.at[:, other_rows], hsend, hrecv, device(x, zh, zl, y, 1 - c)).wait_recv()
 
@@ -409,7 +418,7 @@
             shape((T, D), BF),
         ],
         in_specs=[vmem] * 10,
-        out_specs=[vmem, anywhere, vmem, anywhere, anywhere, anywhere, vmem, vmem, vmem, anywhere],
+        out_specs=[anywhere] * 6 + [vmem] + [anywhere] * 3,
         scratch_shapes=[
             pltpu.VMEM((8, 16, 128), BF),
             pltpu.VMEM((16, 128), BF),
@@ -417,6 +426,10 @@
             pltpu.VMEM((128, 2 * FS), BF),
             pltpu.VMEM((PAD, D), BF),
             pltpu.VMEM((T, 128), BF),
+            pltpu.VMEM((TEAM, ROWS, D), BF),
+            pltpu.VMEM((D, 384), BF),
+            pltpu.VMEM((T, 384), F32),
+            pltpu.VMEM((T, 128), F32),
             pltpu.SemaphoreType.DMA((3, 9)),
             pltpu.SemaphoreType.DMA((3, 9)),
             pltpu.SemaphoreType.DMA((5, 7)),
@@ -424,6 +437,7 @@
             pltpu.SemaphoreType.DMA((8,)),
             pltpu.SemaphoreType.DMA(()),
             pltpu.SemaphoreType.DMA(()),
+            pltpu.SemaphoreType.DMA((4,)),
         ],
         compiler_params=pltpu.CompilerParams(
             collective_id=collective_id, has_side_effects=True, vmem_limit_bytes=VLIM
@@ -459,7 +473,7 @@
     def add_pair(self, s):
         share, b = self.share, self.mine[s]
         half = ROWS // 2
-        self.pairs[s].wait()
+        self.pairs[s].wait_recv()
         total = share[b].astype(F32) + self.pair_land[s].astype(F32)
         if s in (1, 2):
             self.hops[s - 1].wait_recv()
@@ -479,6 +493,8 @@
                 self.hops[1].start()
 
     def result(self):
+        for pair in self.pairs:
+            pair.wait_send()
         for k in (0, 1):
             self.hops[k].wait_send()
         for k in (2, 3):
@@ -501,7 +517,7 @@
 
 def ffn_kernel(
     tok_hbm, e_hbm, z_hbm, w_out_hbm, w_gu_hbm, w_down_hbm, gain_ref,
-    block_out, dh1_out, do_hbm, gu_both, down_both, gain_grad,
+    block_out, dh1_out, do_hbm, gu_both, d_down_hbm, gain_grad,
     tok, e, z, w_out, w_gu, w_down, n2, a, dgq, h1_ref, do_own, share, local, wlocal, blocal,
     dsend, drecv, pair_land, half_land, land, psend, precv, send, recv, *rings,
 ):
@@ -510,17 +526,21 @@
         pltpu.make_async_copy(src, dst, wlocal.at[i])
         for i, (src, dst) in enumerate(((w_out_hbm, w_out), (w_gu_hbm, w_gu), (w_down_hbm, w_down)))
     ]
+    right, left, across = 2 * ((y + 1) % 4), 2 * ((y + 3) % 4), 2 * ((y + 2) % 4)
+    order = ((across, across + 1), (right, left), (right + 1, left + 1), (2 * y, 2 * y + 1))
     blocks = []
-    for s, turn in enumerate((2, 1, 3, 0)):
-        k = (y + turn) % 4
-        pair, rows = pl.ds(2 * k, 2), pl.ds(pl.multiple_of(2 * ROWS * k, 2 * ROWS), 2 * ROWS)
-        blocks.append(
-            [
-                pltpu.make_async_copy(z_hbm.at[rows], z.at[s % 2], blocal.at[s, 0]),
-                pltpu.make_async_copy(tok_hbm.at[pair], tok.at[s % 2], blocal.at[s, 1]),
-                pltpu.make_async_copy(e_hbm.at[pair], e.at[pair], blocal.at[s, 2]),
-            ]
-        )
+    for s, pair in enumerate(order):
+        copies = []
+        for i, b in enumerate(pair):
+            rows = pl.ds(pl.multiple_of(ROWS * b, ROWS), ROWS)
+            copies.append(
+                [
+                    pltpu.make_async_copy(z_hbm.at[rows], z.at[s % 2, pl.ds(i * ROWS, ROWS)], blocal.at[s, i, 0]),
+                    pltpu.make_async_copy(tok_hbm.at[b], tok.at[s % 2, i], blocal.at[s, i, 1]),
+                    pltpu.make_async_copy(e_hbm.at[b], e.at[b], blocal.at[s, i, 2]),
+                ]
+            )
+        blocks.append([copies[0][0], copies[1][0], copies[0][1], copies[1][1], copies[0][2], copies[1][2]])
     weights[0].start()
     for copy in blocks[0]:
         copy.start()
@@ -528,10 +548,10 @@
         copy.start()
     for s, copies in enumerate(blocks[1:]):
         for i, copy in enumerate(copies):
-            if i == 2 or s == 0:
+            if i >= 4 or s == 0:
                 copy.start()
     meet(team_peers() + x_peers())
-    gu, down = RingSum(w_gu, *rings[:4]), RingSum(w_down, *rings[4:])
+    gu = RingSum(w_gu, *rings)
     sums = [
         TeamSum(
             share.at[k], pair_land.at[k], half_land.at[k], land.at[k],
@@ -552,48 +572,80 @@
                 for copy in blocks[k]:
                     copy.wait()
                 if k in (1, 2):
-                    for copy in blocks[k + 1][:2]:
+                    for copy in blocks[k + 1][:4]:
                         copy.start()
 
-        chip = (y + pick(s, (2, 1, 3, 0))) % 4
-        rows = pl.ds(pl.multiple_of(2 * ROWS * chip, 2 * ROWS), 2 * ROWS)
+        both = [pick(s, [pair[i] for pair in order]) for i in range(2)]
+        places = [pl.ds(pl.multiple_of(b * ROWS, ROWS), ROWS) for b in both]
         h1 = tok[s % 2].reshape(2 * ROWS, D).astype(F32) + dot(z[s % 2], w_out[...])
         h1_ref[...] = h1.reshape(2, ROWS, D)
         n2_b = (h1 * rms_scale(h1) * gain).astype(BF)
-        n2[rows, :] = n2_b
+        for i in range(2):
+            n2[places[i], :] = n2_b[i * ROWS : (i + 1) * ROWS]
         g = dot(n2_b, w_gu[:, :, :FS].reshape(D, FS))
         q = dot(n2_b, w_gu[:, :, FS:].reshape(D, FS))
         sig = jax.nn.sigmoid(g)
         act = g * sig
-        a[rows, :] = (act * q).astype(BF)
-        da = back_project(e[pl.ds(2 * chip, 2)].reshape(2 * ROWS, D), w_down[...].reshape(FS, D))
-        dgq[rows, :FS] = (da * q * sig * (1.0 + g * (1.0 - sig))).astype(BF)
-        dgq[rows, FS:] = (da * act).astype(BF)
-        for k in range(1, 4):
+        a_b = (act * q).astype(BF)
+        e_b = jnp.concatenate([e[both[0]], e[both[1]]], axis=0)
+        da = back_project(e_b, w_down[...].reshape(FS, D))
+        dg = (da * q * sig * (1.0 + g * (1.0 - sig))).astype(BF)
+        dq = (da * act).astype(BF)
+        for i in range(2):
+            half = slice(i * ROWS, (i + 1) * ROWS)
+            a[places[i], :] = a_b[half]
+            dgq[places[i], :FS] = dg[half]
+            dgq[places[i], FS:] = dq[half]
+
+        @pl.when(s == 1)
+        def _():
+            sums[0].add_pair(0)
+
+        @pl.when((s == 2) & (c == 0))
+        def _():
+            sums[0].add_pair(1)
+            sums[0].add_pair(2)
+
+        @pl.when((s == 3) & (c == 1))
+        def _():
+            sums[0].add_pair(1)
+            sums[0].add_pair(2)
+
+        for i in range(2):
+            dn2 = back_project(dgq[places[i], :], w_gu[...].reshape(D, 2 * FS))
+            share[0, both[i]] = dn2.astype(BF)
+            h1 = h1_ref[i]
+            gain_grad[...] += jnp.sum(dn2 * (h1 * rms_scale(h1)), axis=0, keepdims=True)
+            share[1, both[i]] = dot(a[places[i], :], w_down[...].reshape(FS, D)).astype(BF)
+
+        for k in (0, 3):
 
             @pl.when(s == k)
             def _():
-                sums[0].add_pair(k - 1)
-
-        for own in range(2):
-            core = c if own else 1 - c
-            b = 2 * chip + core
-            block = pl.ds(pl.multiple_of(b * ROWS, ROWS), ROWS)
-            dn2 = back_project(dgq[block, :], w_gu[...].reshape(D, 2 * FS))
-            share[0, b] = dn2.astype(BF)
-            h1 = h1_ref[core]
-            gain_grad[...] += jnp.sum(dn2 * (h1 * rms_scale(h1)), axis=0, keepdims=True)
-            share[1, b] = dot(a[block, :], w_down[...].reshape(FS, D)).astype(BF)
-            for k in range(4):
-
-                @pl.when(s == k)
-                def _():
-                    if own:
-                        if k:
-                            sums[1].add_pair(k - 1)
-                    else:
-                        sums[0].send_pair(k)
-                        sums[1].send_pair(k)
+                for job in sums:
+                    job.send_pair(k)
+
+        for core in range(2):
+
+            @pl.when((s == 1 + core) & (c != core))
+            def _():
+                for job in sums:
+                    job.send_pair(1)
+                    job.send_pair(2)
+
+        @pl.when(s == 1)
+        def _():
+            sums[1].add_pair(0)
+
+        @pl.when((s == 2) & (c == 0))
+        def _():
+            sums[1].add_pair(1)
+            sums[1].add_pair(2)
+
+        @pl.when((s == 3) & (c == 1))
+        def _():
+            sums[1].add_pair(1)
+            sums[1].add_pair(2)
 
         return carry
 
@@ -613,8 +665,9 @@
     lax.fori_loop(0, 2, tile, 0)
     sums[0].add_pair(3)
     w_down[...] = contract_rows(a[...], e[...].reshape(T, D)).astype(BF).reshape(8, PAD, D)
+    d_down_out = pltpu.make_async_copy(w_down, d_down_hbm, wlocal.at[2])
+    d_down_out.start()
     gu.near_out()
-    down.far_out()
     dn2 = sums[0].result()
     h1 = h1_ref[c]
     dh1 = e[2 * y + c].astype(F32) + norm_reverse(h1, rms_scale(h1), gain, dn2)
@@ -623,14 +676,12 @@
     do_job = TeamGather(do_own, block_part(do_hbm), dsend, drecv, local)
     do_job.start()
     sums[1].add_pair(3)
-    down.near_out()
     do_job.step()
     block_out[...] = (h1_ref[c] + sums[1].result()).astype(BF)
     do_job.finish()
     gu.totals(gu_both)
-    down.totals(down_both)
     gu.finish()
-    down.finish()
+    d_down_out.wait()
 
 
 def ffn(tok, e, z, w_out, w_gu, w_down, gain, collective_id, name):
@@ -643,11 +694,11 @@
             shape((ROWS, D), F32),
             shape((TEAM, ROWS, D), BF),
             shape((2, 128, 2 * FS), BF),
-            shape((2, PAD, D), BF),
+            shape((8, PAD, D), BF),
             shape((1, D), F32),
         ],
         in_specs=[anywhere] * 6 + [vmem],
-        out_specs=[vmem, vmem, anywhere, vmem, vmem, vmem],
+        out_specs=[vmem, vmem, anywhere, vmem, anywhere, vmem],
         scratch_shapes=[
             pltpu.VMEM((2, 2, ROWS, D), BF),
             pltpu.VMEM((TEAM, ROWS, D), BF),
@@ -663,13 +714,12 @@
             pltpu.VMEM((2, TEAM, ROWS, D), BF),
             pltpu.SemaphoreType.DMA(()),
             pltpu.SemaphoreType.DMA((3,)),
-            pltpu.SemaphoreType.DMA((4, 3)),
+            pltpu.SemaphoreType.DMA((4, 2, 3)),
             pltpu.SemaphoreType.DMA((9,)),
             pltpu.SemaphoreType.DMA((9,)),
         ]
         + TeamSum.scratch(2)
-        + RingSum.scratch(128, 2 * FS, BF)
-        + RingSum.scratch(PAD, D, BF),
+        + RingSum.scratch(128, 2 * FS, BF),
         compiler_params=pltpu.CompilerParams(
             collective_id=collective_id, has_side_effects=True, vmem_limit_bytes=VLIM
         ),
@@ -678,9 +728,9 @@
 
 
 def conv_back_kernel(
-    tok_hbm, do_hbm, z_hbm, w_out_hbm, gu_both, down_both, w_in, p, v, dh1, gains, gain_two_grad,
+    tok_hbm, do_hbm, z_hbm, w_out_hbm, gu_both, d_down, w_in, p, v, dh1, gains, gain_two_grad,
     token_grad, gu_out, down_out, in_out, out_out, small_out,
-    tok, do, z, d_in, d_out, d_small, in_both, out_both, small_both, w_out_t, n1, up, dv, dp, sums, share, local, *rest,
+    tok, do, z, d_in, d_out, d_small, down_both, in_both, out_both, small_both, w_out_t, n1, up, dv, dp, sums, share, local, *rest,
 ):
     x, zh, zl, y, c = coords()
     member = 2 * y + c
@@ -699,16 +749,16 @@
     for copy in loads:
         copy.start()
     dn1_sum = TeamSum(share, *[ref.at[0] for ref in rest[:7]])
-    in_ring, out_ring, small_ring = [
-        RingSum(ref, *rest[7 + 4 * i : 11 + 4 * i]) for i, ref in enumerate((d_in, d_out, d_small))
+    down_ring, in_ring, out_ring, small_ring = [
+        RingSum(ref, *rest[7 + 4 * i : 11 + 4 * i]) for i, ref in enumerate((d_down, d_in, d_out, d_small))
     ]
     parts = (
         (gu_both, gu_out), (down_both, down_out), (in_both, in_out), (out_both, out_out), (small_both, small_out)
     )
-    jobs = [PartnerSum(*part, *rest[19 + 7 * i : 26 + 7 * i]) for i, part in enumerate(parts)]
+    jobs = [PartnerSum(*part, *rest[23 + 7 * i : 30 + 7 * i]) for i, part in enumerate(parts)]
     gu, down, in_job, out_job, small = jobs
     gu.z_out()
-    down.z_out()
+    down_ring.far_out()
     loads[0].wait()
     loads[1].wait()
     taps = gains[:, pl.ds(pl.multiple_of(member * 128, 128), 128)]
@@ -744,8 +794,8 @@
         return carry
 
     lax.fori_loop(0, 8, second, 0)
+    down_ring.near_out()
     gu.z_lo_out()
-    down.z_lo_out()
     def third(i, carry):
         s, own = i // 2, i % 2
         turn = jnp.where(s == 0, 2, jnp.where(s == 1, 1, jnp.where(s == 2, 3, 0)))
@@ -762,17 +812,20 @@
             def _():
                 dn1_sum.send_pair(k)
 
-            @pl.when(i == 2 * k + 1)
+            @pl.when(i == 2 * k + 2)
             def _():
                 dn1_sum.add_pair(k)
 
         return carry
 
     lax.fori_loop(0, 8, third, 0)
+    down_ring.totals(down_both)
+    down.z_out()
     gu.team_out()
+    dn1_sum.add_pair(3)
     d_in[...] = contract_rows(n1[...], dp[...]).astype(BF).reshape(8, 128, 384)
     in_ring.far_out()
-    down.team_out()
+    down.z_lo_out()
     loads[3].wait()
     d_out[...] = (
         contract_rows(z[...], do[:, :, pl.ds(pl.multiple_of(member * 128, 128), 128)].reshape(T, 128))
@@ -780,6 +833,7 @@
         .reshape(8, 128, 128)
     )
     out_ring.far_out()
+    down.team_out()
     conv = sums[2:5, :128]
     for g in range(8):
         d_small[g] = jnp.zeros((16, 128), F32)
@@ -816,7 +870,7 @@
     for job in jobs:
         job.gather.near_done()
         job.gather.far_done()
-    for ring in (out_ring, in_ring, small_ring):
+    for ring in (down_ring, out_ring, in_ring, small_ring):
         ring.finish()
 
 
@@ -835,7 +889,7 @@
         pltpu.VMEM((T, D), BF),
     ]
     scratch += [pltpu.VMEM((8,) + block, kind) for block, kind in blocks[2:]]
-    scratch += [pltpu.VMEM((2,) + block, kind) for block, kind in blocks[2:]]
+    scratch += [pltpu.VMEM((2,) + block, kind) for block, kind in blocks[1:]]
     scratch += [
         pltpu.VMEM((128, D), BF),
         pltpu.VMEM((T, D), BF),
@@ -847,7 +901,7 @@
         pltpu.SemaphoreType.DMA((4,)),
     ]
     scratch += TeamSum.scratch(1)
-    for block, kind in blocks[2:]:
+    for block, kind in blocks[1:]:
         scratch += RingSum.scratch(*block, kind)
     for block, kind in blocks:
         scratch += PartnerSum.scratch(*block, kind)
@@ -870,6 +924,7 @@
             at = part * D + 128 * t
             g_in[:, at : at + 128] = w_in[t, :, 128 * part : 128 * part + 128].astype(F32)
         g_out[:, 128 * t : 128 * t + 128] = w_out[t].astype(F32)
+    for t in range(2):
         g_down[SEG * t : SEG * t + SEG, :] = down[t, :SEG].astype(F32)
     total = small[0]
     for t in range(1, TEAM):
@@ -879,22 +934,26 @@
     g_conv[...] = total[2:5]
     b_out[...] = block[...]
     t_out[...] = token[...]
-
-    def chunk(i, carry):
-        rows = pl.ds(pl.multiple_of(i * 32, 32), 32)
-        pieces = [gu[t, rows].astype(F32) for t in range(TEAM)]
-        for half, ref in ((0, g_gate), (FS, g_up)):
-            for g in range(8):
-                for t in range(TEAM):
-                    at = 576 * g + SEG * t
-                    ref[rows, at : at + SEG] = pieces[t][:, half + PAD * g : half + PAD * g + SEG]
-        return carry
-
-    lax.fori_loop(0, 4, chunk, 0)
+    pieces = [gu[t].astype(F32) for t in range(TEAM)]
+    for half, ref in ((0, g_gate), (FS, g_up)):
+        for g in range(8):
+            for t in range(TEAM):
+                at = 576 * g + SEG * t
+                ref[:, at : at + SEG] = pieces[t][:, half + PAD * g : half + PAD * g + SEG]
 
 
 def assemble(gu, down, w_in, w_out, small, block, token):
-    vmem, shape = pl.BlockSpec(memory_space=pltpu.VMEM), jax.ShapeDtypeStruct
+    shape = jax.ShapeDtypeStruct
+
+    def rows(count, width):
+        return pl.BlockSpec((count, width), lambda i: (i, 0))
+
+    def members(count, width):
+        return pl.BlockSpec((TEAM, count, width), lambda i: (0, i, 0))
+
+    def whole(*dims):
+        return pl.BlockSpec(dims, lambda i: (0,) * len(dims))
+
     return pl.pallas_call(
         assemble_kernel,
         out_shape=[
@@ -909,8 +968,28 @@
             shape((ROWS, D), BF),
             shape((ROWS, D), F32),
         ],
-        in_specs=[vmem] * 7,
-        out_specs=[vmem] * 10,
+        grid=(4,),
+        in_specs=[
+            members(32, 2 * FS),
+            pl.BlockSpec((2, PAD, D), lambda i: (i, 0, 0)),
+            members(32, 384),
+            members(32, 128),
+            whole(TEAM, 16, 128),
+            rows(64, D),
+            rows(64, D),
+        ],
+        out_specs=[
+            rows(32, 3 * D),
+            rows(32, D),
+            rows(32, 8 * 576),
+            rows(32, 8 * 576),
+            rows(144, D),
+            whole(1, 128),
+            whole(1, 128),
+            whole(3, 128),
+            rows(64, D),
+            rows(64, D),
+        ],
         compiler_params=pltpu.CompilerParams(vmem_limit_bytes=VLIM),
         name="assemble",
     )(gu, down, w_in, w_out, small, block, token)
@@ -949,9 +1028,9 @@
         "front",
     )
     w_out = w_out.reshape(D, D)
-    block_out, dh1, do, gu_both, down_both, d_gain_two = ffn(tok, e, z, w_out, w_gu, w_down, gains, 1, "ffn")
+    block_out, dh1, do, gu_both, d_down, d_gain_two = ffn(tok, e, z, w_out, w_gu, w_down, gains, 1, "ffn")
     token_grad, s_gu, s_down, s_in, s_out, s_small = conv_back(
-        (tok, do, z, w_out, gu_both, down_both, w_in, p, v, dh1, gains, d_gain_two), 2, "conv_back"
+        (tok, do, z, w_out, gu_both, d_down, w_in, p, v, dh1, gains, d_gain_two), 2, "conv_back"
     )
     g_in, g_out, g_gate, g_up, g_down, g_one, g_two, g_conv, block_out, token_grad = assemble(
         s_gu, s_down, s_in, s_out, s_small, block_out, token_grad

time: 245 us -> 231 us (0.943)
  Pallas kernels: 244 us -> 230 us
    pallas_call x1, Pallas kernels: 79.5 us -> 74.1 us  [conv_back(): pl.pallas_call(conv_back_kernel, out_shape=[shape((ROWS, D), F32)] + [sha...]
    pallas_call x1, Pallas kernels: 80.7 us -> 76.1 us  [ffn(): pl.pallas_call(ffn_kernel, out_shape=[shape((ROWS, D), BF), shape((ROWS,...]
    pallas_call x1, Pallas kernels: 74.9 us -> 72.1 us  [front(): pl.pallas_call(front_kernel, out_shape=[shape((TEAM, ROWS, D), BF), shape...]
where the time goes in v4:
time: 231 us
  Pallas kernels  230 us (100%)
    pallas_call x1, Pallas kernels, ffn(): pl.pallas_call(ffn_kernel, out_shape=[shape((ROWS, D), BF), shape((ROWS,...  76.1 us
    pallas_call x1, Pallas kernels, conv_back(): pl.pallas_call(conv_back_kernel, out_shape=[shape((ROWS, D), F32)] + [sha...  74.1 us
    pallas_call x1, Pallas kernels, front(): pl.pallas_call(front_kernel, out_shape=[shape((TEAM, ROWS, D), BF), shape...  72.1 us
    pallas_call x1, Pallas kernels, assemble(): pl.pallas_call(assemble_kernel, out_shape=[shape((128, 3 * D), F32), shap...  7.6 us

profile of v4, /device:TPU:1, one launch (start us, length us, event | category | flops | bytes accessed | tf_op | source)
XLA Modules:
  0.0 230.6 jit_solution(9145124747285337443)
XLA Ops:
  0.6 72.1 %front.1 = (bf16[8,256,1024]{2,1,0:T(8,128)(2,1)}, bf16[8,256,1024]{2,1,0:T(8,128)(2,1)}, bf16[1024,384]{1,0:T(8,128)(2,1)}, bf16[8,128,1024]{2,1,0:T(8,128)(2,1...) custom-call(bf16[256,1024]{1,0:T(8,128)(2,1)} %tokens.1, ...), custom_call_target="tpu_custom_call" | custom-call | tf_op jit(solution)/shard_map/front/pallas_call | solution.py:406
  72.7 76.1 %ffn.1 = (bf16[256,1024]{1,0:T(8,128)(2,1)}, f32[256,1024]{1,0:T(8,128)}, bf16[8,256,1024]{2,1,0:T(8,128)(2,1)}, bf16[2,128,1280]{2,1,0:T(8,128)(2,1)}, bf16[8,80,1024]{2,1,0:T(8,128)(2,1)}, /*index=5*/f32[1,1024]{1,0:T(1,128)}) custom-call(bf16[8,256,1024]{2,1,0:T(8,128)(2,1)} %get-tuple-element.42.tok_hbm, bf16[8,256,1024]{2,1,0:T(8,128)(2,1)} %get-tuple-element.43.e_hbm, ...), custom_call_target="tpu_custom_call" | custom-call | tf_op jit(solution)/shard_map/ffn/pallas_call | solution.py:690
  148.8 74.1 %conv_back.1 = (f32[256,1024]{1,0:T(8,128)}, bf16[8,128,1280]{2,1,0:T(8,128)(2,1)}, bf16[8,80,1024]{2,1,0:T(8,128)(2,1)}, bf16[8,128,384]{2,1,0:T(8,128)(2,1)}, ...) custom-call(bf16[8,256,1024]{2,1,0:T(8,128)(2,1)} %get-tuple-element.42.tok_hbm, ...), custom_call_target="tpu_custom_call" | custom-call | tf_op jit(solution)/shard_map/conv_back/pallas_call | solution.py:908
  222.9 7.6 %assemble.1 = (f32[128,3072]{1,0:T(8,128)}, f32[128,1024]{1,0:T(8,128)}, f32[128,4608]{1,0:T(8,128)}, f32[128,4608]{1,0:T(8,128)}, f32[576,1024]{1,0:T(8,128)}, ...) custom-call(bf16[8,128,1280]{2,1,0:T(8,128)(2,1)} %get-tuple-element, ...), custom_call_target="tpu_custom_call" | custom-call | tf_op jit(solution)/shard_map/assemble/pallas_call | solution.py:957

commit v5 on v4

--- a/solution.py
+++ b/solution.py
@@ -816,12 +816,15 @@
             def _():
                 dn1_sum.add_pair(k)
 
+        @pl.when(i == 5)
+        def _():
+            gu.team_out()
+
         return carry
 
     lax.fori_loop(0, 8, third, 0)
     down_ring.totals(down_both)
     down.z_out()
-    gu.team_out()
     dn1_sum.add_pair(3)
     d_in[...] = contract_rows(n1[...], dp[...]).astype(BF).reshape(8, 128, 384)
     in_ring.far_out()

time: 231 us -> 230 us (level)
  no operation moved by 1% of the time
where the time goes in v5:
time: 230 us; the launch traced here: 229 us
  Pallas kernels  229 us (100%)
    pallas_call x1, Pallas kernels, ffn(): pl.pallas_call(ffn_kernel, out_shape=[shape((ROWS, D), BF), shape((ROWS,...  76.1 us
    pallas_call x1, Pallas kernels, conv_back(): pl.pallas_call(conv_back_kernel, out_shape=[shape((ROWS, D), F32)] + [sha...  72.9 us
    pallas_call x1, Pallas kernels, front(): pl.pallas_call(front_kernel, out_shape=[shape((TEAM, ROWS, D), BF), shape...  72.1 us
    pallas_call x1, Pallas kernels, assemble(): pl.pallas_call(assemble_kernel, out_shape=[shape((128, 3 * D), F32), shap...  7.6 us

profile of v5, /device:TPU:1, one launch (start us, length us, event | category | flops | bytes accessed | tf_op | source)
XLA Modules:
  0.0 229.5 jit_solution(10898908139221750022)
XLA Ops:
  0.6 72.1 %front.1 = (bf16[8,256,1024]{2,1,0:T(8,128)(2,1)}, bf16[8,256,1024]{2,1,0:T(8,128)(2,1)}, bf16[1024,384]{1,0:T(8,128)(2,1)}, bf16[8,128,1024]{2,1,0:T(8,128)(2,1...) custom-call(bf16[256,1024]{1,0:T(8,128)(2,1)} %tokens.1, ...), custom_call_target="tpu_custom_call" | custom-call | tf_op jit(solution)/shard_map/front/pallas_call | solution.py:406
  72.7 76.1 %ffn.1 = (bf16[256,1024]{1,0:T(8,128)(2,1)}, f32[256,1024]{1,0:T(8,128)}, bf16[8,256,1024]{2,1,0:T(8,128)(2,1)}, bf16[2,128,1280]{2,1,0:T(8,128)(2,1)}, bf16[8,80,1024]{2,1,0:T(8,128)(2,1)}, /*index=5*/f32[1,1024]{1,0:T(1,128)}) custom-call(bf16[8,256,1024]{2,1,0:T(8,128)(2,1)} %get-tuple-element.42.tok_hbm, bf16[8,256,1024]{2,1,0:T(8,128)(2,1)} %get-tuple-element.43.e_hbm, ...), custom_call_target="tpu_custom_call" | custom-call | tf_op jit(solution)/shard_map/ffn/pallas_call | solution.py:690
  148.8 72.9 %conv_back.1 = (f32[256,1024]{1,0:T(8,128)}, bf16[8,128,1280]{2,1,0:T(8,128)(2,1)}, bf16[8,80,1024]{2,1,0:T(8,128)(2,1)}, bf16[8,128,384]{2,1,0:T(8,128)(2,1)}, ...) custom-call(bf16[8,256,1024]{2,1,0:T(8,128)(2,1)} %get-tuple-element.42.tok_hbm, ...), custom_call_target="tpu_custom_call" | custom-call | tf_op jit(solution)/shard_map/conv_back/pallas_call | solution.py:911
  221.7 7.6 %assemble.1 = (f32[128,3072]{1,0:T(8,128)}, f32[128,1024]{1,0:T(8,128)}, f32[128,4608]{1,0:T(8,128)}, f32[128,4608]{1,0:T(8,128)}, f32[576,1024]{1,0:T(8,128)}, ...) custom-call(bf16[8,128,1280]{2,1,0:T(8,128)(2,1)} %get-tuple-element, ...), custom_call_target="tpu_custom_call" | custom-call | tf_op jit(solution)/shard_map/assemble/pallas_call | solution.py:960
